TPU v7x, 32 devices: a whole 2x2x4 slice. The times are simulated.
32 devices in a mesh: row: 8 (over y, x, core), col: 4 (over z).
Axes of the slice: x: 2, y: 2, z: 4, core: 2. Of those that a mesh axis runs over, the one named last changes fastest.
Arguments:
- documents: bfloat16 [2, 4096, 2048], P(None, ('row', 'col')), may hold values from -6 to 6
- targets: bfloat16 [2, 4096, 2048], P(None, ('row', 'col')), may hold values from -6 to 6
- routes: int32 [2, 4096, 1], P(None, ('row', 'col')), may hold values from 0 to 31; in each aligned block of 128 rows (0 to 127, 128 to 255, ..., all dimensions but the last counted through in order) at most 8 rows name the same one
- doc_counts: int32 [8, 4], replicated, may hold values from 1 to 64
- module_one: float32 [8, 2048, 2048], P('row', 'col'), may hold values from -6 to 6
- module_two: float32 [4, 2048, 2048], P('col', 'row'), may hold values from -6 to 6
- moment_one: float32 [8, 2048, 2048], P('row', 'col'), may hold values from -0.75 to 0.75
- moment_two: float32 [4, 2048, 2048], P('col', 'row'), may hold values from -0.75 to 0.75
Outputs:
- new_one: float32 [8, 2048, 2048], P('row', 'col')
- new_two: float32 [4, 2048, 2048], P('col', 'row')
- next_moment_one: float32 [8, 2048, 2048], P('row', 'col')
- next_moment_two: float32 [4, 2048, 2048], P('col', 'row')
Inputs may be any that keep to these rules, and one draw needn't show every extreme that they name: `routes`: in each micro-batch, at most 8 of the 128 rows that one device holds name the same path.
All inputs are finite; a program needn't handle non-finite values.
Results may differ from a plain program's by a relative error of at most 0.011.
Values may be sent and summed in bfloat16 or wider, within the bound.
No kernel may reach another device: no remote copies, remote signals or barrier semaphores. Data moves between devices by JAX's collectives and lax.ppermute only.
A program may use at most 192 MiB of HBM per device.

v0:
```python
import functools

import jax
import jax.numpy as jnp
from jax import lax
from jax.experimental import pallas as pl
from jax.experimental.pallas import tpu as pltpu
from jax.sharding import PartitionSpec as P

beta_one = 0.9
beta_two = 0.95
inner_rate = 0.1
decay = 0.1
outer_rate = 0.7
outer_moment = 0.9

STEP_VMEM = 56 * 1024 * 1024
TILE_VMEM = 32 * 1024 * 1024
f32 = jnp.float32
bf16 = jnp.bfloat16


def step_kernel(rows_dev, tile, keep, base, one_at, two_at, *refs):
    n_one, n_two = len(one_at), len(two_at)
    place_ref, xy_ref = refs[:2]
    refs = refs[2:]

    def take(places):
        nonlocal refs
        found = [tuple(refs[sum(p[1] for p in places[:i]) :][: p[1]]) for i, p in enumerate(places)]
        refs = refs[sum(p[1] for p in places) :]
        return found

    one_refs, two_refs = take(one_at), take(two_at)
    left_ref, right_ref = refs[:2]
    start_out = refs[2] if keep else None
    one, two, pre, one_sem, two_sem, out_sem = refs[-6:]
    width = one.shape[0]
    scale = width ** (-0.5)
    parts = width // tile
    home = place_ref[base + n_one + n_two]

    class Copies:
        def __init__(self, *choices):
            self.choices = choices

        def start(self):
            if len(self.choices) == 1:
                self.choices[0].start()
            else:
                pl.when(home == 1)(self.choices[0].start)
                pl.when(home == 0)(self.choices[1].start)

        def wait(self):
            self.choices[0].wait()

    def one_copies(n):
        found = []
        for i, (pieces, (first, _, top, tall)) in enumerate(zip(one_refs, one_at)):
            wide = pieces[0].shape[1]
            if first <= n * tile < first + wide:
                down = pl.ds(pl.multiple_of(place_ref[base + i] * tall, tall), tall)
                found.append(
                    Copies(*[
                        pltpu.make_async_copy(
                            piece.at[pl.ds(top, tall), pl.ds(n * tile - first, tile)],
                            one.at[down, pl.ds(n * tile, tile)],
                            one_sem.at[i, n],
                        )
                        for piece in pieces
                    ])
                )
        return found

    two_copies = []
    for i, (pieces, (first, _, top, tall)) in enumerate(zip(two_refs, two_at)):
        wide = pieces[0].shape[1]
        down = pl.ds(pl.multiple_of(place_ref[base + n_one + i] * tall, tall), tall)
        two_copies.append(
            Copies(*[
                pltpu.make_async_copy(piece.at[pl.ds(top, tall), :], two.at[down, pl.ds(first, wide)], two_sem.at[i])
                for piece in pieces
            ])
        )
    for n in range(parts):
        for copy in one_copies(n):
            copy.start()
    for copy in two_copies:
        copy.start()
    for n in range(parts):
        span = pl.ds(n * tile, tile)
        for copy in one_copies(n):
            copy.wait()
        value = jnp.dot(xy_ref[:, :width], one[:, span], preferred_element_type=f32) * scale
        pre[:, span] = value
        left_ref[:, span] = xy_ref[:, span]
        left_ref[:, pl.ds(width + n * tile, tile)] = (value * jax.nn.sigmoid(value)).astype(bf16)
    for copy in two_copies:
        copy.wait()
    if keep:
        one_save = pltpu.make_async_copy(one, start_out.at[pl.ds(0, width), :], out_sem.at[0])
        two_save = pltpu.make_async_copy(two, start_out.at[pl.ds(width, width), :], out_sem.at[1])
        one_save.start()
        two_save.start()

    def miss(n, carry):
        span = pl.ds(pl.multiple_of(n * tile, tile), tile)
        late = pl.ds(pl.multiple_of(width + n * tile, tile), tile)
        out = xy_ref[:, span].astype(f32) + jnp.dot(left_ref[:, width:], two[:, span], preferred_element_type=f32) * scale
        right_ref[:, late] = ((out - xy_ref[:, late].astype(f32)) / rows_dev).astype(bf16)
        return carry

    lax.fori_loop(0, parts, miss, 0, unroll=True)

    def backward(n, carry):
        span = pl.ds(pl.multiple_of(n * tile, tile), tile)
        back = lax.dot_general(
            right_ref[:, width:], two[span, :], (((1,), (1,)), ((), ())), preferred_element_type=f32
        ) * scale
        value = pre[:, span]
        sig = jax.nn.sigmoid(value)
        right_ref[:, span] = (back * (sig * (1.0 + value * (1.0 - sig)))).astype(bf16)
        return carry

    lax.fori_loop(0, parts, backward, 0, unroll=True)
    if keep:
        one_save.wait()
        two_save.wait()


def step(xy, one, two, rows_dev, keep, places, base):
    rows, width = xy.shape[0], xy.shape[1] // 2
    tile = 1024
    vmem = pl.BlockSpec(memory_space=pltpu.VMEM)
    hbm = pl.BlockSpec(memory_space=pl.ANY)
    out = jax.ShapeDtypeStruct((rows, 2 * width), bf16)
    whole = jax.ShapeDtypeStruct((2 * width, width), bf16)
    sources = [array for p in one + two for array in p[0]]

    def entries(pieces):
        return tuple((p[1], len(p[0]), *(p[2:] or (0, p[0][0].shape[0]))) for p in pieces)

    return pl.pallas_call(
        functools.partial(
            step_kernel, rows_dev, tile, keep, base, entries(one), entries(two)
        ),
        out_shape=(out, out) + ((whole,) if keep else ()),
        in_specs=[pl.BlockSpec(memory_space=pltpu.SMEM), vmem] + [hbm] * len(sources),
        out_specs=(vmem, vmem) + ((hbm,) if keep else ()),
        scratch_shapes=[
            pltpu.VMEM((width, width), bf16),
            pltpu.VMEM((width, width), bf16),
            pltpu.VMEM((rows, width), f32),
            pltpu.SemaphoreType.DMA((len(one), width // tile)),
            pltpu.SemaphoreType.DMA((len(two),)),
            pltpu.SemaphoreType.DMA((2,)),
        ],
        compiler_params=pltpu.CompilerParams(vmem_limit_bytes=STEP_VMEM if keep else TILE_VMEM),
        cost_estimate=pl.CostEstimate(flops=15 * rows * width * width, bytes_accessed=4 * width * width, transcendentals=0),
    )(places, xy, *sources)


def update_kernel(guard, tile, a_ref, b_ref, p_ref, out_ref):
    shrink = inner_rate * decay
    turned = a_ref[...].T
    for n in range(p_ref.shape[1] // tile):
        span = slice(n * tile, (n + 1) * tile)
        grad = jnp.dot(turned, b_ref[:, span], preferred_element_type=f32)
        move = grad * pl.reciprocal(jnp.abs(grad) + guard, approx=True)
        out_ref[:, span] = (p_ref[:, span].astype(f32) * (1.0 - shrink) - inner_rate * move).astype(bf16)


def update(left, right, start, guard):
    rows, width = left.shape[0], start.shape[1]
    tall = 512
    each = width // tall
    return pl.pallas_call(
        functools.partial(update_kernel, guard * width ** 0.5, 512),
        out_shape=jax.ShapeDtypeStruct(start.shape, bf16),
        grid=(2 * each,),
        in_specs=[
            pl.BlockSpec((rows, tall), lambda m: (0, m)),
            pl.BlockSpec((rows, width), lambda m: (0, m // each)),
            pl.BlockSpec((tall, width), lambda m: (m, 0)),
        ],
        out_specs=pl.BlockSpec((tall, width), lambda m: (m, 0)),
        compiler_params=pltpu.CompilerParams(vmem_limit_bytes=TILE_VMEM),
        cost_estimate=pl.CostEstimate(flops=12 * rows * width * start.shape[0], bytes_accessed=4 * start.size, transcendentals=0),
    )(left, right, start)


def term_kernel(guard, tile, base, spans, place_ref, weight_ref, a_ref, b_ref, c_ref, d_ref, p_ref, *refs):
    outs, held, sem = refs[:-2], refs[-2], refs[-1]
    step = pl.program_id(0)
    slot = step % 2
    last = spans[-1][1]
    short, wide = p_ref.shape

    def copies(m, slot):
        return [
            (
                (m >= begin) & (m < end),
                pltpu.make_async_copy(
                    held.at[slot], out.at[pl.ds(pl.multiple_of((m - begin) * short, short), short), :], sem.at[slot]
                ),
            )
            for out, (begin, end) in zip(outs, spans)
        ]

    def settle(slot):
        pltpu.make_async_copy(held.at[slot], outs[0].at[pl.ds(0, short), :], sem.at[slot]).wait()

    @pl.when(step >= 2)
    def _():
        settle(slot)

    weight = jnp.where(place_ref[base + 3 * last + step] == 0, weight_ref[0], weight_ref[1])
    shrink = inner_rate * decay
    new_m = (1.0 - beta_one) / (1.0 - beta_one ** 2)
    new_v = ((1.0 - beta_two) / (1.0 - beta_two ** 2)) ** 0.5
    by_first = weight * (inner_rate * (1.0 - shrink))
    by_second = weight * (inner_rate * new_m / new_v)
    by_start = weight * (shrink * (2.0 - shrink))
    older, newer = a_ref[...].T, c_ref[...].T
    for n in range(wide // tile):
        span = slice(n * tile, (n + 1) * tile)
        old = jnp.dot(older, b_ref[:, span], preferred_element_type=f32)
        new = jnp.dot(newer, d_ref[:, span], preferred_element_type=f32)
        first = old * pl.reciprocal(jnp.abs(old) + guard, approx=True)
        square = beta_two * (old * old) + new * new
        root = square * lax.rsqrt(square + 1e-30)
        second = (beta_one * old + new) * pl.reciprocal(root + guard / new_v, approx=True)
        start = p_ref[:, span].astype(f32)
        held[slot, :, span] = (first * by_first + second * by_second + start * by_start).astype(bf16)
    for here, copy in copies(step, slot):
        pl.when(here)(copy.start)

    @pl.when(step == last - 1)
    def _():
        settle(slot)
        if last > 1:
            settle(1 - slot)


def terms(weights, places, base, counts, short, parts, a, b, c, d, p, guard):
    rows, width = a.shape[0], p.shape[1]
    wide = width // parts
    ends = [sum(counts[: n + 1]) for n in range(len(counts))]
    spans = tuple((end - count, end) for count, end in zip(counts, ends))
    last = ends[-1]
    row = lambda m, at: at[base + m]
    col = lambda m, at: at[base + last + m]
    both = lambda m, at: at[base + 2 * last + m]
    side = pl.BlockSpec((rows, short), lambda m, at: (0, row(m, at)))
    full = pl.BlockSpec((rows, wide), lambda m, at: (0, both(m, at)))
    return pl.pallas_call(
        functools.partial(term_kernel, guard * width ** 0.5, 256, base, spans),
        out_shape=tuple(jax.ShapeDtypeStruct((count * short, wide), bf16) for count in counts),
        grid_spec=pltpu.PrefetchScalarGridSpec(
            num_scalar_prefetch=1,
            grid=(last,),
            in_specs=[
                pl.BlockSpec(memory_space=pltpu.SMEM),
                side, full, side, full,
                pl.BlockSpec((short, wide), lambda m, at: (row(m, at), col(m, at))),
            ],
            out_specs=tuple(pl.BlockSpec(memory_space=pl.ANY) for _ in counts),
            scratch_shapes=[pltpu.VMEM((2, short, wide), bf16), pltpu.SemaphoreType.DMA((2,))],
        ),
        compiler_params=pltpu.CompilerParams(vmem_limit_bytes=TILE_VMEM),
        cost_estimate=pl.CostEstimate(flops=1, bytes_accessed=1, transcendentals=0),
    )(places, weights, a, b, c, d, p)


def slots(routes, documents, targets, device_of, room):
    dest = device_of(routes[:, 0])
    paths = device_of(None)
    hit = (dest[:, None] == jnp.arange(paths, dtype=jnp.int32)[None, :]).astype(jnp.int32)
    before = jnp.cumsum(hit, axis=0) - hit
    slot = dest * room + jnp.sum(before * hit, axis=1)
    place = (slot[:, None] == jnp.arange(paths * room, dtype=jnp.int32)[None, :]).astype(bf16)
    both = jnp.concatenate([documents, targets], axis=1)
    return jnp.einsum("rs,rd->sd", place, both, preferred_element_type=f32).astype(bf16)


def after(value, *others):
    return lax.optimization_barrier((value,) + others)[0]


def shards(documents, targets, routes, doc_counts, module_one, module_two, moment_one, moment_two):
    n_row = lax.axis_size("row")
    n_col = lax.axis_size("col")
    chips, half = n_row // 2, n_col // 2
    paths = n_row * n_col
    row_id = lax.axis_index("row")
    col_id = lax.axis_index("col")
    chip, core = row_id // 2, row_id % 2
    side, turn = col_id // half, col_id % half
    home = core == side
    micro, rows_dev, width = documents.shape
    room = max(2, 2 * rows_dev // paths)
    guard = 0.5 / (width * rows_dev) ** 0.5

    def device_of(path):
        if path is None:
            return paths
        i, j = path // n_col, path % n_col
        return (2 * (i // 2) + j // half) * n_col + (i % 2) * half + j % half

    def send(value, target):
        pairs = []
        for i in range(n_row):
            for k in range(n_col):
                to = target(i // 2, i % 2, k // half, k % half)
                if to is not None:
                    c, b, h, q = to
                    pairs.append((i * n_col + k, (2 * c + b) * n_col + h * half + q))
        return lax.ppermute(value, ("row", "col"), pairs)

    def to_core(value):
        return send(value, lambda c, b, h, q: (c, 1 - b, h, q))

    def to_turn(value, s):
        return send(value, lambda c, b, h, q: (c, b, h, (q + s) % half))

    def to_chip(value, bit):
        return send(value, lambda c, b, h, q: (c ^ bit, b, h, q))

    bits = [1 << t for t in range(chips.bit_length() - 1)]
    orders = [bits, bits[::-1]]
    cols = width // 2

    every = list(range(chips))
    tall_one, tall_two = width // n_col, width // chips
    short = min(tall_one, tall_two, 512)
    table = []

    def enter(*pieces):
        talls = (tall_one, tall_two)
        listed = [
            (
                level * (width // short) + block * (talls[level] // short) + cut,
                part,
                level * 2 + part,
                level,
            )
            for level, blocks, part in pieces
            for block in blocks
            for cut in range(talls[level] // short)
        ]
        base = len(table)
        for field in zip(*listed):
            table.extend(field)
        return base, tuple(len(blocks) * (talls[level] // short) for level, blocks, part in pieces)

    here = [(turn + s) % half + core * half for s in range(half)]
    there = [(turn + s) % half + (1 - core) * half for s in range(half)]
    leave = [[chip ^ r for r in every if r & order[0]] for order in orders]
    stay = [[chip ^ r for r in every if not r & order[0]] for order in orders]
    calls = [
        enter((0, there, 0), (0, there, 1)),
        enter((0, here, 0), (0, here, 1)),
        enter((1, leave[0], 0), (1, leave[1], 1)),
        enter((1, stay[0], 0), (1, stay[1], 1)),
    ]
    base_first = len(table)
    for part in range(2):
        for other in (core, 1 - core):
            table += [(turn - s) % half + other * half for s in range(half)]
    for order in orders:
        held = [0]
        for bit in order:
            held = held + [r ^ bit for r in held]
        table += [chip ^ r for r in held]
    table.append(home)
    base_second = len(table)
    table += [0, 0, 0]
    places = jnp.stack([jnp.asarray(value).astype(jnp.int32) for value in table])

    counts = doc_counts.astype(f32)
    path_one, path_two = 2 * chip + side, turn + core * half
    in_row = (jnp.arange(n_row) == path_one)[:, None]
    in_col = (jnp.arange(n_col) == path_two)[None, :]
    row_counts = jnp.sum(jnp.where(in_row, counts, 0.0))
    col_counts = jnp.sum(jnp.where(in_col, counts, 0.0))
    own_count = jnp.sum(jnp.where(in_row & in_col, counts, 0.0))
    weights = jnp.stack([own_count / row_counts, own_count / col_counts])

    sent = [slots(routes[s], documents[s], targets[s], device_of, room) for s in range(micro)]

    def exchange(value):
        return lax.all_to_all(
            value.reshape(paths, room, 2 * width), ("row", "col"), split_axis=0, concat_axis=0, tiled=True
        ).reshape(paths * room, 2 * width)

    own_two = module_two[0].astype(bf16)
    own_one = module_one[0].astype(bf16)
    other_two = send(own_two, lambda c, b, h, q: (c, h, h, q) if b != h else None)
    pair_two = jnp.where(
        core == 0,
        jnp.concatenate([own_two, other_two], axis=0),
        jnp.concatenate([other_two, own_two], axis=0),
    )

    def to_chips(value, bit, here):
        return send(value, lambda c, b, h, q: (c ^ bit, b, h, q) if (b == h) == here else None)

    def to_half(value, here):
        if half == 1:
            return jnp.zeros_like(value)
        return send(value, lambda c, b, h, q: (c, b, h, (q + 1) % half) if (b == h) == here else None)

    def begin(pair, here):
        own = [pair[:, part * cols : (part + 1) * cols] for part in range(2)]
        return [(value, to_chips(value, order[0], here)) for value, order in zip(own, orders)]

    def proceed(held, here):
        for n in range(1, len(bits)):
            held = [jnp.concatenate(pieces, axis=0) for pieces in held]
            held = [(value, to_chips(value, order[n], here)) for value, order in zip(held, orders)]
        return held

    def barrier(*values):
        return jax.tree.unflatten(jax.tree.structure(values), lax.optimization_barrier(jax.tree.leaves(values)))

    ones = [own_one[:, :cols], own_one[:, cols:]]

    def far_half(value):
        return send(value, lambda c, b, h, q: (c, 1 - b, 1 - h, q) if b != h else None)

    fars, nears = [far_half(ones[0])], [to_half(ones[0], True)]
    home_two = begin(pair_two, True)
    ones, fars, nears, pair_two, places, weights, sent = barrier(
        ones, fars, nears, pair_two, places, weights, sent
    )
    far_two = send(pair_two, lambda c, b, h, q: (c, b, 1 - h, q) if b == h else None)
    turns = [to_half(fars[0], False)]
    home_two = proceed(home_two, True)
    ones, fars, nears, turns, far_two, home_two, sent = barrier(ones, fars, nears, turns, far_two, home_two, sent)
    fars.append(far_half(ones[1]))
    nears.append(to_half(ones[1], True))
    away_two = begin(far_two, False)
    fars, nears, away_two, sent = barrier(fars, nears, away_two, sent)
    got_a = exchange(sent[0])
    turns.append(to_half(fars[1], False))
    away_two = proceed(away_two, False)
    one = []
    for part in range(2):
        held = [jnp.where(home, ones[part], fars[part])]
        if half > 1:
            held.append(jnp.where(home, nears[part], turns[part]))
        held += [to_turn(held[0], s) for s in range(2, half)]
        joined = jnp.concatenate(held, axis=0)
        for value in (joined, to_core(joined)):
            one += [((value,), part * cols, s * tall_one, tall_one) for s in range(half)]
    two = []
    for part in range(2):
        for mine, theirs in zip(home_two[part], away_two[part]):
            count = mine.shape[0] // tall_two
            two += [((mine, theirs), part * cols, n * tall_two, tall_two) for n in range(count)]
    got_b = exchange(after(sent[1], got_a, away_two[0][1], away_two[1][1]))
    left_a, right_a, start = step(got_a, one, two, rows_dev, True, places, base_first)
    moved = update(left_a, right_a, start, guard)
    left_b, right_b = step(got_b, [((moved,), 0, 0, width)], [((moved,), 0, width, width)], rows_dev, False, places, base_second)

    def deltas(call, *others):
        return terms(after(weights, *others), places, *call, short, 2, left_a, right_a, left_b, right_b, start, guard)

    def summed(*values):
        return functools.reduce(lambda x, y: x + y, [value.astype(f32) for value in values])

    def both_cores(here, there):
        there = to_core(there)
        cuts = [slice(s * tall_one, (s + 1) * tall_one) for s in range(half)]
        return [(here[cut], there[cut]) for cut in cuts]

    def along(both, sums):
        return [*both[0], *[to_turn(value, s) for s, value in enumerate(sums, 1)]]

    def to_owner(terms, *others):
        return send(
            after(summed(*terms).astype(bf16), *others),
            lambda c, b, h, q: (c, 1 - b, 1 - h, q) if b != h else None,
        )

    def chip_sum(part, here, there):
        there = to_chip(there, orders[part][0])
        cuts = [slice(n * tall_two, (n + 1) * tall_two) for n in range(chips // 2)]
        left = [r for r in every if not r & orders[part][0]]
        return {r: [here[cut], there[cut]] for r, cut in zip(left, cuts)}

    def chip_rest(part, held, *others):
        held = {r: list(pieces) for r, pieces in held.items()}
        for bit in orders[part][1:]:
            for r in [r for r in sorted(held) if r & bit]:
                held[r ^ bit].append(to_chip(after(summed(*held.pop(r)).astype(bf16), *others), bit))
        return held[0]

    def half_sum(terms, *others):
        total = summed(*terms)
        up, down = total[: tall_two // 2], total[tall_two // 2 :]
        near = send(
            jnp.where(core == 0, down, up).astype(bf16),
            lambda c, b, h, q: (c, 1 - b, h, q) if b == h else None,
        )
        fars = [
            send(
                after(rows.astype(bf16), *others),
                lambda c, b, h, q, to=to: (c, to, 1 - h, q) if b != h else None,
            )
            for to, rows in enumerate((up, down))
        ]
        return jnp.where(home, jnp.where(core == 0, up, down), near.astype(f32)) + jnp.where(
            core == 0, *[far.astype(f32) for far in fars]
        )

    def outer(module, moment, sums):
        average = jnp.concatenate(sums, axis=1)[None]
        following = outer_moment * moment + average
        return module - outer_rate * (outer_moment * following + average), following

    there_a, there_b = deltas(calls[0])
    here_a, here_b = deltas(calls[1], there_a)
    both_a, both_b = both_cores(here_a, there_a), both_cores(here_b, there_b)
    sums_a, sums_b = ([summed(*pair).astype(bf16) for pair in both[1:]] for both in (both_a, both_b))
    leave_a, leave_b = deltas(calls[2], here_a, *sums_a, *sums_b)
    along_a, along_b = along(both_a, sums_a), along(both_b, sums_b)
    stay_a, stay_b = deltas(calls[3], leave_a, along_a[-1])
    owned_a = to_owner(along_a)
    owned_b = to_owner(along_b, stay_a)
    chip_a, chip_b = chip_sum(0, stay_a, leave_a), chip_sum(1, stay_b, leave_b)
    chip_a, chip_b = chip_rest(0, chip_a, owned_a), chip_rest(1, chip_b, owned_a)
    sums_one = [
        jnp.where(home, summed(*terms), owned.astype(f32))
        for terms, owned in ((along_a, owned_a), (along_b, owned_b))
    ]
    new_one, next_moment_one = outer(module_one, moment_one, sums_one)
    sums_two = [half_sum(terms, owned_b) for terms in (chip_a, chip_b)]
    new_two, next_moment_two = outer(module_two, moment_two, sums_two)
    return (new_one, new_two, next_moment_one, next_moment_two)


def solution(mesh):
    return jax.shard_map(
        shards,
        mesh=mesh,
        in_specs=(
            P(None, ("row", "col"), None),
            P(None, ("row", "col"), None),
            P(None, ("row", "col"), None),
            P(),
            P("row", "col", None),
            P("col", "row", None),
            P("row", "col", None),
            P("col", "row", None),
        ),
        out_specs=(
            P("row", "col", None),
            P("col", "row", None),
            P("row", "col", None),
            P("col", "row", None),
        ),
        check_vma=False,
    )
```

profile of v0, /device:TPU:1, one launch (start us, length us, event | category | flops | bytes accessed | tf_op | source)
XLA Modules:
  0.0 403.7 jit_solution(3345350799521855262)
XLA Ops:
  0.6 2.5 convert_bitcast_fusion
  3.1 1.5 fusion.22
  4.7 1.8 collective-permute-start.1
  6.4 5.6 %collective-permute-start = (bf16[512,1024]{1,0:T(8,128)(2,1)}, bf16[512,1024]{1,0:T(8,128)(2,1)}, u32[]{:S(2)}, u32[]{:S(2)}) collective-permute-start(bf16[512,1024]{1,0:T(8,128)(2,1)} %get-tuple-element.75), channel_id=1, source_target_pairs={{2,4},{3,5},{4,2},{5,3},{10,12},{11,13},{12,10},{13,11},{18,20},{1... | collective-permute-start | bytes 3145736 | tf_op jit(solution)/shard_map/ppermute | solution.py:318
  12.2 2.3 collective-permute-start.2
  17.2 2.5 maximum_select_fusion
  21.0 1.6 collective-permute-start.5
  27.8 3.3 convolution_convert_fusion
  31.1 2.1 convolution_convert_fusion.1
  33.3 2.8 collective-permute-done
  36.1 1.3 collective-permute-start.4
  37.4 1.4 pad_maximum_fusion.refs_10_.refs_12_
  39.8 1.6 pad_maximum_fusion.1.refs_18_.refs_20_
  42.2 2.4 collective-permute-start.3
  44.6 23.3 %collective-permute-done.3 = bf16[512,1024]{1,0:T(8,128)(2,1)S(1)} collective-permute-done((bf16[512,1024]{1,0:T(8,128)(2,1)}, bf16[512,1024]{1,0:T(8,128)(2,1)S(1)}, u32[]{:S(2)}, u32[]{:S(2)}) %collective-permute-start.3) | collective-permute-done | bytes 1048608 | tf_op jit(solution)/shard_map/ppermute | solution.py:318
  68.0 18.3 %collective-permute-done.4 = bf16[512,2048]{1,0:T(8,128)(2,1)S(1)} collective-permute-done((bf16[512,2048]{1,0:T(8,128)(2,1)S(1)}, bf16[512,2048]{1,0:T(8,128)(2,1)S(1)}, u32[]{:S(2)}, u32[]{:S(2)}) %collective-permute-start.4) | collective-permute-done | bytes 2097184 | tf_op jit(solution)/shard_map/ppermute | solution.py:318
  87.7 1.9 collective-permute-start.9
  89.8 3.2 collective-permute-start.12
  93.0 3.1 collective-permute-start.11
  96.1 19.8 %collective-permute-done.9 = bf16[512,1024]{1,0:T(8,128)(2,1)S(1)} collective-permute-done((bf16[512,1024]{1,0:T(8,128)(2,1)S(1)}, bf16[512,1024]{1,0:T(8,128)(2,1)S(1)}, u32[]{:S(2)}, u32[]{:S(2)}) %collective-permute-start.9) | collective-permute-done | bytes 1048608 | tf_op jit(solution)/shard_map/ppermute | solution.py:318
  118.2 4.2 %all-to-all-start = ((bf16[32,8,4096]{2,1,0:T(8,128)(2,1)}), bf16[32,8,4096]{2,1,0:T(8,128)(2,1)}, u32[]{:S(2)}, u32[]{:S(2)}) async-start(bf16[32,8,4096]{2,1,0:T(8,128)(2,1)} %bitcast.75), calls=%async_computation | async-start | bytes 4194304 | tf_op jit(solution)/shard_map/all_to_all | solution.py:392
  122.4 3.4 collective-permute-start.14
  126.2 3.4 collective-permute-start.17
  129.6 3.1 collective-permute-start.16
  132.7 1.6 broadcast_select_fusion.2
  134.3 1.5 pad_maximum_fusion.2.refs_2_.refs_3_
  135.9 34.9 %collective-permute-done.14 = bf16[512,1024]{1,0:T(8,128)(2,1)S(1)} collective-permute-done((bf16[512,1024]{1,0:T(8,128)(2,1)}, bf16[512,1024]{1,0:T(8,128)(2,1)S(1)}, u32[]{:S(2)}, u32[]{:S(2)}) %collective-permute-start.14) | collective-permute-done | bytes 1048608 | tf_op jit(solution)/shard_map/ppermute | solution.py:318
  171.0 1.5 pad_maximum_fusion.3.refs_6_.refs_7_
  172.5 1.3 copy-done.35
  173.8 4.5 %all-to-all-start.1 = ((bf16[32,8,4096]{2,1,0:T(8,128)(2,1)}), bf16[32,8,4096]{2,1,0:T(8,128)(2,1)S(1)}, u32[]{:S(2)}, u32[]{:S(2)}) async-start(bf16[32,8,4096]{2,1,0:T(8,128)(2,1)} %bitcast.74), calls=%async_computation.1 | async-start | bytes 4194304 | tf_op jit(solution)/shard_map/all_to_all | solution.py:392
  178.3 16.6 %shard_map.111 = (bf16[256,4096]{1,0:T(8,128)(2,1)}, bf16[256,4096]{1,0:T(8,128)(2,1)}, bf16[4096,2048]{1,0:T(8,128)(2,1)}) custom-call(s32[84]{0:T(128)} %stack.94.refs_0_.place_ref, bf16[256,4096]{1,0:T(8,128)(2,1)} %bitcast.26.refs_1_, bf16[1024,1024]{1,0:T(8,128)(2,1)} %pad_maximum_fusion.2.refs_2_.refs_3_, ...), custom_call_target="tpu_custom_call" | custom-call | flops 16106127360 | bytes 16777216 | tf_op jit(solution)/shard_map/pallas_call | solution.py:143
  194.9 1.6 copy-done
  196.5 1.6 copy-done.2
  198.1 14.1 %shard_map.112.refs_2_.refs_3_ = bf16[4096,2048]{1,0:T(8,128)(2,1)S(1)} custom-call(bf16[256,4096]{1,0:T(8,128)(2,1)S(1)} %copy-done, bf16[256,4096]{1,0:T(8,128)(2,1)S(1)} %copy-done.2, bf16[4096,2048]{1,0:T(8,128)(2,1)} %get-tuple-element.93.p_ref), custom_call_target="tpu_custom_call" | custom-call | flops 25769803776 | bytes 33554432 | tf_op jit(solution)/shard_map/pallas_call | solution.py:177
  212.2 5.7 %copy-done.5 = bf16[4096,2048]{1,0:T(8,128)(2,1)} copy-done((bf16[4096,2048]{1,0:T(8,128)(2,1)}, bf16[4096,2048]{1,0:T(8,128)(2,1)S(1)}, u32[]{:S(2)}) %copy-start.5) | copy-done | bytes 16777240
  217.9 8.5 %all-to-all-done.1 = bf16[32,8,4096]{2,1,0:T(8,128)(2,1)S(1)} async-done(((bf16[32,8,4096]{2,1,0:T(8,128)(2,1)}), bf16[32,8,4096]{2,1,0:T(8,128)(2,1)S(1)}, u32[]{:S(2)}, u32[]{:S(2)}) %all-to-all-start.1) | async-done | bytes 2097184 | tf_op jit(solution)/shard_map/all_to_all | solution.py:392
  226.5 11.8 %shard_map.113 = (bf16[256,4096]{1,0:T(8,128)(2,1)S(1)}, bf16[256,4096]{1,0:T(8,128)(2,1)S(1)}) custom-call(s32[84]{0:T(128)S(1)} %copy-done.4, bf16[256,4096]{1,0:T(8,128)(2,1)S(1)} %bitcast.73, bf16[4096,2048]{1,0:T(8,128)(2,1)} %copy-done.5, bf16[4096,2048]{1,0:T(8,128)(2,1)} %copy-done.5), custom_call_target="tpu_custom_call" | custom-call | flops 16106127360 | bytes 16777216 | tf_op jit(solution)/shard_map/pallas_call | solution.py:143
  238.3 9.7 %shard_map.114 = (bf16[1024,1024]{1,0:T(8,128)(2,1)S(1)}, bf16[1024,1024]{1,0:T(8,128)(2,1)S(1)}) custom-call(s32[84]{0:T(128)S(1)} %copy-done.4, f32[2]{0:T(128)S(1)} %pad_maximum_fusion.4.weight_ref, bf16[256,4096]{1,0:T(8,128)(2,1)S(1)} %copy-done.1, bf16[256,4096]{1,0:T(8,128)(2,1)S(1)} %copy-done.3, bf16[256,4096]{1,0:T(8,128)(2,1)S(1)} %get-tuple-element.94.c_ref, ...), custom_call_target="tpu_custom_call" | custom-call | flops 1 | bytes 1 | tf_op jit(solution)/shard_map/pallas_call | solution.py:256
  248.6 9.7 %shard_map.115 = (bf16[1024,1024]{1,0:T(8,128)(2,1)S(1)}, bf16[1024,1024]{1,0:T(8,128)(2,1)S(1)}) custom-call(s32[84]{0:T(128)S(1)} %copy-done.4, f32[2]{0:T(128)S(1)} %pad_maximum_fusion.4.weight_ref, bf16[256,4096]{1,0:T(8,128)(2,1)S(1)} %copy-done.1, bf16[256,4096]{1,0:T(8,128)(2,1)S(1)} %copy-done.3, bf16[256,4096]{1,0:T(8,128)(2,1)S(1)} %get-tuple-element.94.c_ref, ...), custom_call_target="tpu_custom_call" | custom-call | flops 1 | bytes 1 | tf_op jit(solution)/shard_map/pallas_call | solution.py:256
  258.7 2.0 collective-permute-start.19
  260.7 1.4 add_convert_fusion.2
  262.1 10.0 %shard_map.116 = (bf16[1024,1024]{1,0:T(8,128)(2,1)S(1)}, bf16[1024,1024]{1,0:T(8,128)(2,1)S(1)}) custom-call(s32[84]{0:T(128)S(1)} %copy-done.4, f32[2]{0:T(128)S(1)} %pad_maximum_fusion.4.weight_ref, bf16[256,4096]{1,0:T(8,128)(2,1)S(1)} %copy-done.1, bf16[256,4096]{1,0:T(8,128)(2,1)S(1)} %copy-done.3, bf16[256,4096]{1,0:T(8,128)(2,1)S(1)} %get-tuple-element.94.c_ref, ...), custom_call_target="tpu_custom_call" | custom-call | flops 1 | bytes 1 | tf_op jit(solution)/shard_map/pallas_call | solution.py:256
  273.9 10.0 %collective-permute-done.19 = bf16[512,1024]{1,0:T(8,128)(2,1)S(1)} collective-permute-done((bf16[512,1024]{1,0:T(8,128)(2,1)S(1)}, bf16[512,1024]{1,0:T(8,128)(2,1)S(1)}, u32[]{:S(2)}, u32[]{:S(2)}) %collective-permute-start.19) | collective-permute-done | bytes 1048608 | tf_op jit(solution)/shard_map/ppermute | solution.py:318
  283.9 1.6 fusion
  285.5 4.1 %collective-permute-start.20 = (bf16[512,1024]{1,0:T(8,128)(2,1)}, bf16[512,1024]{1,0:T(8,128)(2,1)S(1)}, u32[]{:S(2)}, u32[]{:S(2)}) collective-permute-start(bf16[512,1024]{1,0:T(8,128)(2,1)} %fusion), channel_id=1, source_target_pairs={{2,4},{3,5},{4,2},{5,3},{10,12},{11,13},{12,10},{13,11},{18,20},{1... | collective-permute-start | bytes 3145736 | tf_op jit(solution)/shard_map/ppermute | solution.py:318
  289.6 9.7 %shard_map.117 = (bf16[1024,1024]{1,0:T(8,128)(2,1)S(1)}, bf16[1024,1024]{1,0:T(8,128)(2,1)S(1)}) custom-call(s32[84]{0:T(128)S(1)} %copy-done.4, f32[2]{0:T(128)S(1)} %pad_maximum_fusion.4.weight_ref, bf16[256,4096]{1,0:T(8,128)(2,1)S(1)} %copy-done.1, bf16[256,4096]{1,0:T(8,128)(2,1)S(1)} %copy-done.3, bf16[256,4096]{1,0:T(8,128)(2,1)S(1)} %get-tuple-element.94.c_ref, ...), custom_call_target="tpu_custom_call" | custom-call | flops 1 | bytes 1 | tf_op jit(solution)/shard_map/pallas_call | solution.py:256
  299.3 18.3 %collective-permute-done.22 = bf16[512,1024]{1,0:T(8,128)(2,1)S(1)} collective-permute-done((bf16[512,1024]{1,0:T(8,128)(2,1)}, bf16[512,1024]{1,0:T(8,128)(2,1)S(1)}, u32[]{:S(2)}, u32[]{:S(2)}) %collective-permute-start.22) | collective-permute-done | bytes 1048608 | tf_op jit(solution)/shard_map/ppermute | solution.py:318
  318.2 1.9 collective-permute-start.23
  320.6 1.6 collective-permute-start.30
  322.9 2.2 convert_select_fusion.1
  325.1 20.6 %collective-permute-done.23 = bf16[512,1024]{1,0:T(8,128)(2,1)S(1)} collective-permute-done((bf16[512,1024]{1,0:T(8,128)(2,1)S(1)}, bf16[512,1024]{1,0:T(8,128)(2,1)S(1)}, u32[]{:S(2)}, u32[]{:S(2)}) %collective-permute-start.23) | collective-permute-done | bytes 1048608 | tf_op jit(solution)/shard_map/ppermute | solution.py:318
  345.7 2.2 convert_select_fusion
  349.6 1.8 collective-permute-start.32
  351.3 1.9 collective-permute-start.33
  353.3 1.3 collective-permute-start.31
  356.4 5.5 %collective-permute-start.27 = (bf16[256,1024]{1,0:T(8,128)(2,1)}, bf16[256,1024]{1,0:T(8,128)(2,1)}, u32[]{:S(2)}, u32[]{:S(2)}) collective-permute-start(bf16[256,1024]{1,0:T(8,128)(2,1)} %get-tuple-element.107), channel_id=1, source_target_pairs={{2,0},{3,1},{4,2},{5,3},{10,8},{11,9},{12,10},{13,11},{18,16},{19,... | collective-permute-start | bytes 1572872 | tf_op jit(solution)/shard_map/ppermute | solution.py:318
  361.9 2.2 collective-permute-start.28
  364.1 1.6 collective-permute-start.26
  365.7 8.8 %multiply_subtract_fusion = (f32[1,512,2048]{2,1,0:T(8,128)}, f32[1,512,2048]{2,1,0:T(8,128)}) fusion(f32[1,512,2048]{2,1,0:T(8,128)S(1)} %copy-done.6, f32[512,1024]{1,0:T(8,128)} %convert_select_fusion, f32[512,1024]{1,0:T(8,128)} %convert_select_fusion.1, f32[1,512,2048]{2,1,0:T(8,128)} %param.14), kind=kLoop, calls=%fused_computation.3 | loop fusion | flops 7340032 | bytes 20971520 | tf_op jit(solution)/shard_map/sub | solution.py:520
  374.5 12.9 %collective-permute-done.33 = bf16[256,1024]{1,0:T(8,128)(2,1)S(1)} collective-permute-done((bf16[256,1024]{1,0:T(8,128)(2,1)}, bf16[256,1024]{1,0:T(8,128)(2,1)S(1)}, u32[]{:S(2)}, u32[]{:S(2)}) %collective-permute-start.33) | collective-permute-done | bytes 524320 | tf_op jit(solution)/shard_map/ppermute | solution.py:318
  387.4 1.4 select_add_fusion
  388.9 9.9 %collective-permute-done.28 = bf16[256,1024]{1,0:T(8,128)(2,1)} collective-permute-done((bf16[256,1024]{1,0:T(8,128)(2,1)}, bf16[256,1024]{1,0:T(8,128)(2,1)}, u32[]{:S(2)}, u32[]{:S(2)}) %collective-permute-start.28) | collective-permute-done | bytes 524320 | tf_op jit(solution)/shard_map/ppermute | solution.py:318
  398.7 1.8 select_add_fusion.1
  400.5 2.7 multiply_subtract_fusion.1
  (144 shorter events, 21.0 us)
Async XLA Ops:
  3.1 8.9 %copy-start.7 = (f32[1,256,2048]{2,1,0:T(8,128)S(1)}, f32[1,256,2048]{2,1,0:T(8,128)}, u32[]{:S(2)}) copy-start(f32[1,256,2048]{2,1,0:T(8,128)} %param.13) | copy-start | bytes 6291460
  4.7 9.9 %copy-start.32 = (s32[2,128,1]{1,2,0:T(1,128)S(1)}, s32[2,128,1]{1,2,0:T(1,128)}, u32[]{:S(2)}) copy-start(s32[2,128,1]{1,2,0:T(1,128)} %param.10) | copy-start | bytes 3076
  4.7 10.5 %copy-start.19 = (bf16[2,128,2048]{2,1,0:T(8,128)(2,1)S(1)}, bf16[2,128,2048]{2,1,0:T(8,128)(2,1)}, u32[]{:S(2)}) copy-start(bf16[2,128,2048]{2,1,0:T(8,128)(2,1)} %param.8) | copy-start | bytes 3145732
  4.7 11.5 %copy-start.20 = (bf16[2,128,2048]{2,1,0:T(8,128)(2,1)S(1)}, bf16[2,128,2048]{2,1,0:T(8,128)(2,1)}, u32[]{:S(2)}) copy-start(bf16[2,128,2048]{2,1,0:T(8,128)(2,1)} %param.9) | copy-start | bytes 3145732
  4.7 28.6 %collective-permute-start.1 = (bf16[512,1024]{1,0:T(8,128)(2,1)}, bf16[512,1024]{1,0:T(8,128)(2,1)}, u32[]{:S(2)}, u32[]{:S(2)}) collective-permute-start(bf16[512,1024]{1,0:T(8,128)(2,1)} %get-tuple-element.75), channel_id=1, source_target_pairs={{0,1},{1,0},{6,7},{7,6},{8,9},{9,8},{14,15},{15,14},{16,17},{17,16... | collective-permute-start | bytes 3145736 | tf_op jit(solution)/shard_map/ppermute | solution.py:318
  6.4 29.7 %collective-permute-start = (bf16[512,1024]{1,0:T(8,128)(2,1)}, bf16[512,1024]{1,0:T(8,128)(2,1)}, u32[]{:S(2)}, u32[]{:S(2)}) collective-permute-start(bf16[512,1024]{1,0:T(8,128)(2,1)} %get-tuple-element.75), channel_id=1, source_target_pairs={{2,4},{3,5},{4,2},{5,3},{10,12},{11,13},{12,10},{13,11},{18,20},{1... | collective-permute-start | bytes 3145736 | tf_op jit(solution)/shard_map/ppermute | solution.py:318
  12.2 5.0 %collective-permute-start.2 = (bf16[256,2048]{1,0:T(8,128)(2,1)S(1)}, bf16[256,2048]{1,0:T(8,128)(2,1)}, u32[]{:S(2)}, u32[]{:S(2)}) collective-permute-start(bf16[256,2048]{1,0:T(8,128)(2,1)S(1)} %convert_bitcast_fusion.1), channel_id=1, source_target_pairs={{2,6},{3,7},{4,0},{5,1},{10,14},{11,15},{12,8},{13,9},{18,22},{19,... | collective-permute-start | bytes 3145736 | tf_op jit(solution)/shard_map/ppermute | solution.py:318
  19.7 2.9 copy-start.31
  21.0 16.4 %collective-permute-start.5 = (bf16[512,1024]{1,0:T(8,128)(2,1)S(1)}, bf16[512,1024]{1,0:T(8,128)(2,1)}, u32[]{:S(2)}, u32[]{:S(2)}) collective-permute-start(bf16[512,1024]{1,0:T(8,128)(2,1)S(1)} %get-tuple-element.130), channel_id=1, source_target_pairs={{0,8},{1,9},{6,14},{7,15},{8,0},{9,1},{14,6},{15,7},{16,24},{17,25... | collective-permute-start | bytes 3145736 | tf_op jit(solution)/shard_map/ppermute | solution.py:318
  26.7 4.5 %copy-start.15 = (bf16[128,2048]{1,0:T(8,128)(2,1)S(1)}, bf16[128,2048]{1,0:T(8,128)(2,1)}, u32[]{:S(2)}) copy-start(bf16[128,2048]{1,0:T(8,128)(2,1)} %get-tuple-element.134) | copy-start | bytes 1572868
  26.7 4.5 %copy-start.16 = (bf16[128,2048]{1,0:T(8,128)(2,1)S(1)}, bf16[128,2048]{1,0:T(8,128)(2,1)}, u32[]{:S(2)}) copy-start(bf16[128,2048]{1,0:T(8,128)(2,1)} %get-tuple-element.136) | copy-start | bytes 1572868
  26.9 12.9 %collective-permute-start.7 = (bf16[512,1024]{1,0:T(8,128)(2,1)}, bf16[512,1024]{1,0:T(8,128)(2,1)S(1)}, u32[]{:S(2)}, u32[]{:S(2)}) collective-permute-start(bf16[512,1024]{1,0:T(8,128)(2,1)} %get-tuple-element.129), channel_id=1, source_target_pairs={{0,16},{1,17},{6,22},{7,23},{8,24},{9,25},{14,30},{15,31},{16,0},{... | collective-permute-start | bytes 3145736 | tf_op jit(solution)/shard_map/ppermute | solution.py:318
  36.1 50.1 %collective-permute-start.4 = (bf16[512,2048]{1,0:T(8,128)(2,1)S(1)}, bf16[512,2048]{1,0:T(8,128)(2,1)S(1)}, u32[]{:S(2)}, u32[]{:S(2)}) collective-permute-start(bf16[512,2048]{1,0:T(8,128)(2,1)S(1)} %maximum_select_fusion), channel_id=1, source_target_pairs={{0,2},{1,3},{6,4},{7,5},{8,10},{9,11},{14,12},{15,13},{16,18},{17,... | collective-permute-start | bytes 6291464 | tf_op jit(solution)/shard_map/ppermute | solution.py:318
  38.8 2.6 copy-start.13
  38.8 47.4 %copy-start.9 = (bf16[512,1024]{1,0:T(8,128)(2,1)S(1)}, bf16[512,1024]{1,0:T(8,128)(2,1)}, u32[]{:S(2)}) copy-start(bf16[512,1024]{1,0:T(8,128)(2,1)} %get-tuple-element.69) | copy-start | bytes 3145732
  38.8 47.4 %collective-permute-start.6 = (bf16[1024,1024]{1,0:T(8,128)(2,1)S(1)}, bf16[1024,1024]{1,0:T(8,128)(2,1)S(1)}, u32[]{:S(2)}, u32[]{:S(2)}) collective-permute-start(bf16[1024,1024]{1,0:T(8,128)(2,1)S(1)} %pad_maximum_fusion.refs_10_.refs_12_), channel_id=1, source_target_pairs={{0,16},{1,17},{6,22},{7,23},{8,24},{9,25},{14,30},{15,31},{16,0},{... | collective-permute-start | bytes 6291464 | tf_op jit(solution)/shard_map/ppermute | solution.py:318
  41.4 48.4 %copy-start.14 = (bf16[1024,1024]{1,0:T(8,128)(2,1)}, bf16[1024,1024]{1,0:T(8,128)(2,1)S(1)}, u32[]{:S(2)}) copy-start(bf16[1024,1024]{1,0:T(8,128)(2,1)S(1)} %pad_maximum_fusion.1.refs_18_.refs_20_) | copy-start | bytes 6291460
  41.4 44.8 %collective-permute-start.8 = (bf16[1024,1024]{1,0:T(8,128)(2,1)S(1)}, bf16[1024,1024]{1,0:T(8,128)(2,1)S(1)}, u32[]{:S(2)}, u32[]{:S(2)}) collective-permute-start(bf16[1024,1024]{1,0:T(8,128)(2,1)S(1)} %pad_maximum_fusion.1.refs_18_.refs_20_), channel_id=1, source_target_pairs={{0,8},{1,9},{6,14},{7,15},{8,0},{9,1},{14,6},{15,7},{16,24},{17,25... | collective-permute-start | bytes 6291464 | tf_op jit(solution)/shard_map/ppermute | solution.py:318
  42.2 25.7 %collective-permute-start.3 = (bf16[512,1024]{1,0:T(8,128)(2,1)}, bf16[512,1024]{1,0:T(8,128)(2,1)S(1)}, u32[]{:S(2)}, u32[]{:S(2)}) collective-permute-start(bf16[512,1024]{1,0:T(8,128)(2,1)} %collective-permute-done), channel_id=1, source_target_pairs={{2,3},{3,2},{4,5},{5,4},{10,11},{11,10},{12,13},{13,12},{18,19},{1... | collective-permute-start | bytes 3145736 | tf_op jit(solution)/shard_map/ppermute | solution.py:318
  68.0 19.1 %copy-start.17 = (bf16[512,1024]{1,0:T(8,128)(2,1)}, bf16[512,1024]{1,0:T(8,128)(2,1)S(1)}, u32[]{:S(2)}) copy-start(bf16[512,1024]{1,0:T(8,128)(2,1)S(1)} %collective-permute-done.3) | copy-start | bytes 3145732
  86.3 3.5 copy-start.33
  86.3 9.8 %collective-permute-start.10 = (bf16[512,1024]{1,0:T(8,128)(2,1)S(1)}, bf16[512,1024]{1,0:T(8,128)(2,1)S(1)}, u32[]{:S(2)}, u32[]{:S(2)}) collective-permute-start(bf16[512,1024]{1,0:T(8,128)(2,1)S(1)} %copy-done.9), channel_id=1, source_target_pairs={{0,1},{1,0},{6,7},{7,6},{8,9},{9,8},{14,15},{15,14},{16,17},{17,16... | collective-permute-start | bytes 3145736 | tf_op jit(solution)/shard_map/ppermute | solution.py:318
  87.7 28.2 %collective-permute-start.9 = (bf16[512,1024]{1,0:T(8,128)(2,1)S(1)}, bf16[512,1024]{1,0:T(8,128)(2,1)S(1)}, u32[]{:S(2)}, u32[]{:S(2)}) collective-permute-start(bf16[512,1024]{1,0:T(8,128)(2,1)S(1)} %copy-done.9), channel_id=1, source_target_pairs={{2,4},{3,5},{4,2},{5,3},{10,12},{11,13},{12,10},{13,11},{18,20},{1... | collective-permute-start | bytes 3145736 | tf_op jit(solution)/shard_map/ppermute | solution.py:318
  89.8 26.1 %collective-permute-start.12 = (bf16[512,1024]{1,0:T(8,128)(2,1)S(1)}, bf16[512,1024]{1,0:T(8,128)(2,1)S(1)}, u32[]{:S(2)}, u32[]{:S(2)}) collective-permute-start(bf16[512,1024]{1,0:T(8,128)(2,1)S(1)} %get-tuple-element.86), channel_id=1, source_target_pairs={{2,18},{3,19},{4,20},{5,21},{10,26},{11,27},{12,28},{13,29},{18,2}... | collective-permute-start | bytes 3145736 | tf_op jit(solution)/shard_map/ppermute | solution.py:318
  93.0 22.9 %collective-permute-start.11 = (bf16[512,1024]{1,0:T(8,128)(2,1)S(1)}, bf16[512,1024]{1,0:T(8,128)(2,1)S(1)}, u32[]{:S(2)}, u32[]{:S(2)}) collective-permute-start(bf16[512,1024]{1,0:T(8,128)(2,1)S(1)} %get-tuple-element.82), channel_id=1, source_target_pairs={{2,10},{3,11},{4,12},{5,13},{10,2},{11,3},{12,4},{13,5},{18,26},{1... | collective-permute-start | bytes 3145736 | tf_op jit(solution)/shard_map/ppermute | solution.py:318
  96.1 19.8 %copy-start.21 = (bf16[512,1024]{1,0:T(8,128)(2,1)}, bf16[512,1024]{1,0:T(8,128)(2,1)S(1)}, u32[]{:S(2)}) copy-start(bf16[512,1024]{1,0:T(8,128)(2,1)S(1)} %collective-permute-done.10) | copy-start | bytes 3145732
  118.2 55.6 %all-to-all-start = ((bf16[32,8,4096]{2,1,0:T(8,128)(2,1)}), bf16[32,8,4096]{2,1,0:T(8,128)(2,1)}, u32[]{:S(2)}, u32[]{:S(2)}) async-start(bf16[32,8,4096]{2,1,0:T(8,128)(2,1)} %bitcast.75), calls=%async_computation | async-start | bytes 4194304 | tf_op jit(solution)/shard_map/all_to_all | solution.py:392
  122.4 3.6 copy-start.28
  122.4 48.4 %collective-permute-start.14 = (bf16[512,1024]{1,0:T(8,128)(2,1)}, bf16[512,1024]{1,0:T(8,128)(2,1)S(1)}, u32[]{:S(2)}, u32[]{:S(2)}) collective-permute-start(bf16[512,1024]{1,0:T(8,128)(2,1)} %copy-done.23), channel_id=1, source_target_pairs={{2,3},{3,2},{4,5},{5,4},{10,11},{11,10},{12,13},{13,12},{18,19},{1... | collective-permute-start | bytes 3145736 | tf_op jit(solution)/shard_map/ppermute | solution.py:318
  126.0 3.6 copy-start.26
  126.1 6.7 %copy-start.18 = (bf16[512,1024]{1,0:T(8,128)(2,1)S(1)}, bf16[512,1024]{1,0:T(8,128)(2,1)}, u32[]{:S(2)}) copy-start(bf16[512,1024]{1,0:T(8,128)(2,1)} %copy-done.17) | copy-start | bytes 3145732
  126.1 8.2 %copy-start.30 = (bf16[1024,1024]{1,0:T(8,128)(2,1)}, bf16[1024,1024]{1,0:T(8,128)(2,1)S(1)}, u32[]{:S(2)}) copy-start(bf16[1024,1024]{1,0:T(8,128)(2,1)S(1)} %constant_dynamic-update-slice_fusion.2.refs_19_.refs_21_) | copy-start | bytes 6291460
  126.2 46.3 %collective-permute-start.17 = (bf16[1024,1024]{1,0:T(8,128)(2,1)S(1)}, bf16[1024,1024]{1,0:T(8,128)(2,1)S(1)}, u32[]{:S(2)}, u32[]{:S(2)}) collective-permute-start(bf16[1024,1024]{1,0:T(8,128)(2,1)S(1)} %constant_dynamic-update-slice_fusion.2.refs_19_.refs_21_), channel_id=1, source_target_pairs={{2,10},{3,11},{4,12},{5,13},{10,2},{11,3},{12,4},{13,5},{18,26},{1... | collective-permute-start | bytes 6291464 | tf_op jit(solution)/shard_map/ppermute | solution.py:318
  129.6 4.7 %copy-start.29 = (bf16[1024,1024]{1,0:T(8,128)(2,1)}, bf16[1024,1024]{1,0:T(8,128)(2,1)S(1)}, u32[]{:S(2)}) copy-start(bf16[1024,1024]{1,0:T(8,128)(2,1)S(1)} %constant_dynamic-update-slice_fusion.refs_11_.refs_13_) | copy-start | bytes 6291460
  129.6 44.2 %collective-permute-start.16 = (bf16[1024,1024]{1,0:T(8,128)(2,1)S(1)}, bf16[1024,1024]{1,0:T(8,128)(2,1)}, u32[]{:S(2)}, u32[]{:S(2)}) collective-permute-start(bf16[1024,1024]{1,0:T(8,128)(2,1)S(1)} %constant_dynamic-update-slice_fusion.refs_11_.refs_13_), channel_id=1, source_target_pairs={{2,18},{3,19},{4,20},{5,21},{10,26},{11,27},{12,28},{13,29},{18,2}... | collective-permute-start | bytes 6291464 | tf_op jit(solution)/shard_map/ppermute | solution.py:318
  135.8 35.0 %copy-start.22 = (bf16[512,1024]{1,0:T(8,128)(2,1)S(1)}, bf16[512,1024]{1,0:T(8,128)(2,1)}, u32[]{:S(2)}) copy-start(bf16[512,1024]{1,0:T(8,128)(2,1)} %copy-done.21) | copy-start | bytes 3145732
  135.8 42.5 %collective-permute-start.13 = (bf16[1024,1024]{1,0:T(8,128)(2,1)}, bf16[1024,1024]{1,0:T(8,128)(2,1)}, u32[]{:S(2)}, u32[]{:S(2)}) collective-permute-start(bf16[1024,1024]{1,0:T(8,128)(2,1)} %pad_maximum_fusion.2.refs_2_.refs_3_), channel_id=1, source_target_pairs={{0,4},{1,5},{2,6},{3,7},{4,0},{5,1},{6,2},{7,3},{8,12},{9,13},{10,... | collective-permute-start | bytes 6291464 | tf_op jit(solution)/shard_map/ppermute | solution.py:318
  172.5 5.9 %collective-permute-start.15 = (bf16[1024,1024]{1,0:T(8,128)(2,1)}, bf16[1024,1024]{1,0:T(8,128)(2,1)}, u32[]{:S(2)}, u32[]{:S(2)}) collective-permute-start(bf16[1024,1024]{1,0:T(8,128)(2,1)} %pad_maximum_fusion.3.refs_6_.refs_7_), channel_id=1, source_target_pairs={{0,4},{1,5},{2,6},{3,7},{4,0},{5,1},{6,2},{7,3},{8,12},{9,13},{10,... | collective-permute-start | bytes 6291464 | tf_op jit(solution)/shard_map/ppermute | solution.py:318
  173.8 52.6 %all-to-all-start.1 = ((bf16[32,8,4096]{2,1,0:T(8,128)(2,1)}), bf16[32,8,4096]{2,1,0:T(8,128)(2,1)S(1)}, u32[]{:S(2)}, u32[]{:S(2)}) async-start(bf16[32,8,4096]{2,1,0:T(8,128)(2,1)} %bitcast.74), calls=%async_computation.1 | async-start | bytes 4194304 | tf_op jit(solution)/shard_map/all_to_all | solution.py:392
  198.1 28.4 %copy-start.4 = (s32[84]{0:T(128)S(1)}, s32[84]{0:T(128)}, u32[]{:S(2)}) copy-start(s32[84]{0:T(128)} %stack.94.refs_0_.place_ref) | copy-start | bytes 1012
  212.2 5.7 %copy-start.5 = (bf16[4096,2048]{1,0:T(8,128)(2,1)}, bf16[4096,2048]{1,0:T(8,128)(2,1)S(1)}, u32[]{:S(2)}) copy-start(bf16[4096,2048]{1,0:T(8,128)(2,1)S(1)} %shard_map.112.refs_2_.refs_3_) | copy-start | bytes 50331652
  226.5 11.8 %copy-start.1 = (bf16[256,4096]{1,0:T(8,128)(2,1)S(1)}, bf16[256,4096]{1,0:T(8,128)(2,1)}, u32[]{:S(2)}) copy-start(bf16[256,4096]{1,0:T(8,128)(2,1)} %get-tuple-element.89.a_ref) | copy-start | bytes 6291460
  226.5 11.8 %copy-start.3 = (bf16[256,4096]{1,0:T(8,128)(2,1)S(1)}, bf16[256,4096]{1,0:T(8,128)(2,1)}, u32[]{:S(2)}) copy-start(bf16[256,4096]{1,0:T(8,128)(2,1)} %get-tuple-element.90.b_ref) | copy-start | bytes 6291460
  248.0 10.3 %collective-permute-start.18 = (bf16[1024,1024]{1,0:T(8,128)(2,1)S(1)}, bf16[1024,1024]{1,0:T(8,128)(2,1)S(1)}, u32[]{:S(2)}, u32[]{:S(2)}) collective-permute-start(bf16[1024,1024]{1,0:T(8,128)(2,1)S(1)} %get-tuple-element.96), channel_id=1, source_target_pairs={{0,4},{1,5},{2,6},{3,7},{4,0},{5,1},{6,2},{7,3},{8,12},{9,13},{10,... | collective-permute-start | bytes 6291464 | tf_op jit(solution)/shard_map/ppermute | solution.py:318
  248.1 12.6 %collective-permute-start.21 = (bf16[1024,1024]{1,0:T(8,128)(2,1)S(1)}, bf16[1024,1024]{1,0:T(8,128)(2,1)S(1)}, u32[]{:S(2)}, u32[]{:S(2)}) collective-permute-start(bf16[1024,1024]{1,0:T(8,128)(2,1)S(1)} %get-tuple-element.100), channel_id=1, source_target_pairs={{0,4},{1,5},{2,6},{3,7},{4,0},{5,1},{6,2},{7,3},{8,12},{9,13},{10,... | collective-permute-start | bytes 6291464 | tf_op jit(solution)/shard_map/ppermute | solution.py:318
  258.7 25.1 %collective-permute-start.19 = (bf16[512,1024]{1,0:T(8,128)(2,1)S(1)}, bf16[512,1024]{1,0:T(8,128)(2,1)S(1)}, u32[]{:S(2)}, u32[]{:S(2)}) collective-permute-start(bf16[512,1024]{1,0:T(8,128)(2,1)S(1)} %add_convert_fusion.3), channel_id=1, source_target_pairs={{0,1},{1,0},{2,3},{3,2},{4,5},{5,4},{6,7},{7,6},{8,9},{9,8},{10,11... | collective-permute-start | bytes 3145736 | tf_op jit(solution)/shard_map/ppermute | solution.py:318
  272.1 48.1 %collective-permute-start.29 = (bf16[1024,1024]{1,0:T(8,128)(2,1)S(1)}, bf16[1024,1024]{1,0:T(8,128)(2,1)S(1)}, u32[]{:S(2)}, u32[]{:S(2)}) collective-permute-start(bf16[1024,1024]{1,0:T(8,128)(2,1)S(1)} %get-tuple-element.110), channel_id=1, source_target_pairs={{0,16},{1,17},{2,18},{3,19},{4,20},{5,21},{6,22},{7,23},{8,24},{9,... | collective-permute-start | bytes 6291464 | tf_op jit(solution)/shard_map/ppermute | solution.py:318
  272.5 49.7 %collective-permute-start.24 = (bf16[1024,1024]{1,0:T(8,128)(2,1)S(1)}, bf16[1024,1024]{1,0:T(8,128)(2,1)S(1)}, u32[]{:S(2)}, u32[]{:S(2)}) collective-permute-start(bf16[1024,1024]{1,0:T(8,128)(2,1)S(1)} %get-tuple-element.102), channel_id=1, source_target_pairs={{0,8},{1,9},{2,10},{3,11},{4,12},{5,13},{6,14},{7,15},{8,0},{9,1},... | collective-permute-start | bytes 6291464 | tf_op jit(solution)/shard_map/ppermute | solution.py:318
  273.4 44.2 %collective-permute-start.22 = (bf16[512,1024]{1,0:T(8,128)(2,1)}, bf16[512,1024]{1,0:T(8,128)(2,1)S(1)}, u32[]{:S(2)}, u32[]{:S(2)}) collective-permute-start(bf16[512,1024]{1,0:T(8,128)(2,1)} %add_convert_fusion.2), channel_id=1, source_target_pairs={{0,1},{1,0},{2,3},{3,2},{4,5},{5,4},{6,7},{7,6},{8,9},{9,8},{10,11... | collective-permute-start | bytes 3145736 | tf_op jit(solution)/shard_map/ppermute | solution.py:318
  285.5 35.1 %collective-permute-start.20 = (bf16[512,1024]{1,0:T(8,128)(2,1)}, bf16[512,1024]{1,0:T(8,128)(2,1)S(1)}, u32[]{:S(2)}, u32[]{:S(2)}) collective-permute-start(bf16[512,1024]{1,0:T(8,128)(2,1)} %fusion), channel_id=1, source_target_pairs={{2,4},{3,5},{4,2},{5,3},{10,12},{11,13},{12,10},{13,11},{18,20},{1... | collective-permute-start | bytes 3145736 | tf_op jit(solution)/shard_map/ppermute | solution.py:318
  318.2 27.4 %collective-permute-start.23 = (bf16[512,1024]{1,0:T(8,128)(2,1)S(1)}, bf16[512,1024]{1,0:T(8,128)(2,1)S(1)}, u32[]{:S(2)}, u32[]{:S(2)}) collective-permute-start(bf16[512,1024]{1,0:T(8,128)(2,1)S(1)} %fusion.1), channel_id=1, source_target_pairs={{2,4},{3,5},{4,2},{5,3},{10,12},{11,13},{12,10},{13,11},{18,20},{1... | collective-permute-start | bytes 3145736 | tf_op jit(solution)/shard_map/ppermute | solution.py:318
  320.6 27.2 %collective-permute-start.30 = (bf16[512,1024]{1,0:T(8,128)(2,1)S(1)}, bf16[512,1024]{1,0:T(8,128)(2,1)S(1)}, u32[]{:S(2)}, u32[]{:S(2)}) collective-permute-start(bf16[512,1024]{1,0:T(8,128)(2,1)S(1)} %add_convert_fusion), channel_id=1, source_target_pairs={{0,8},{1,9},{2,10},{3,11},{4,12},{5,13},{6,14},{7,15},{8,0},{9,1},... | collective-permute-start | bytes 3145736 | tf_op jit(solution)/shard_map/ppermute | solution.py:318
  322.2 2.9 copy-start.11
  322.6 32.0 %collective-permute-start.25 = (bf16[512,1024]{1,0:T(8,128)(2,1)S(1)}, bf16[512,1024]{1,0:T(8,128)(2,1)S(1)}, u32[]{:S(2)}, u32[]{:S(2)}) collective-permute-start(bf16[512,1024]{1,0:T(8,128)(2,1)S(1)} %add_convert_fusion.1), channel_id=1, source_target_pairs={{0,16},{1,17},{2,18},{3,19},{4,20},{5,21},{6,22},{7,23},{8,24},{9,... | collective-permute-start | bytes 3145736 | tf_op jit(solution)/shard_map/ppermute | solution.py:318
  348.4 6.2 %copy-start.12 = (bf16[1024,1024]{1,0:T(8,128)(2,1)S(1)}, bf16[1024,1024]{1,0:T(8,128)(2,1)}, u32[]{:S(2)}) copy-start(bf16[1024,1024]{1,0:T(8,128)(2,1)} %copy-done.11) | copy-start | bytes 6291460
  349.6 14.5 %collective-permute-start.32 = (bf16[256,1024]{1,0:T(8,128)(2,1)S(1)}, bf16[256,1024]{1,0:T(8,128)(2,1)S(1)}, u32[]{:S(2)}, u32[]{:S(2)}) collective-permute-start(bf16[256,1024]{1,0:T(8,128)(2,1)S(1)} %get-tuple-element.112), channel_id=1, source_target_pairs={{2,0},{3,1},{4,2},{5,3},{10,8},{11,9},{12,10},{13,11},{18,16},{19,... | collective-permute-start | bytes 1572872 | tf_op jit(solution)/shard_map/ppermute | solution.py:318
  351.3 36.1 %collective-permute-start.33 = (bf16[256,1024]{1,0:T(8,128)(2,1)}, bf16[256,1024]{1,0:T(8,128)(2,1)S(1)}, u32[]{:S(2)}, u32[]{:S(2)}) collective-permute-start(bf16[256,1024]{1,0:T(8,128)(2,1)} %get-tuple-element.113), channel_id=1, source_target_pairs={{2,4},{3,5},{4,6},{5,7},{10,12},{11,13},{12,14},{13,15},{18,20},{1... | collective-permute-start | bytes 1572872 | tf_op jit(solution)/shard_map/ppermute | solution.py:318
  353.3 34.2 %collective-permute-start.31 = (bf16[256,1024]{1,0:T(8,128)(2,1)}, bf16[256,1024]{1,0:T(8,128)(2,1)}, u32[]{:S(2)}, u32[]{:S(2)}) collective-permute-start(bf16[256,1024]{1,0:T(8,128)(2,1)} %get-tuple-element.124), channel_id=1, source_target_pairs={{0,4},{1,5},{6,2},{7,3},{8,12},{9,13},{14,10},{15,11},{16,20},{17,... | collective-permute-start | bytes 1572872 | tf_op jit(solution)/shard_map/ppermute | solution.py:318
  354.6 11.1 %copy-start.6 = (f32[1,512,2048]{2,1,0:T(8,128)S(1)}, f32[1,512,2048]{2,1,0:T(8,128)}, u32[]{:S(2)}) copy-start(f32[1,512,2048]{2,1,0:T(8,128)} %param.12) | copy-start | bytes 12582916
  356.4 32.5 %collective-permute-start.27 = (bf16[256,1024]{1,0:T(8,128)(2,1)}, bf16[256,1024]{1,0:T(8,128)(2,1)}, u32[]{:S(2)}, u32[]{:S(2)}) collective-permute-start(bf16[256,1024]{1,0:T(8,128)(2,1)} %get-tuple-element.107), channel_id=1, source_target_pairs={{2,0},{3,1},{4,2},{5,3},{10,8},{11,9},{12,10},{13,11},{18,16},{19,... | collective-permute-start | bytes 1572872 | tf_op jit(solution)/shard_map/ppermute | solution.py:318
  361.9 36.9 %collective-permute-start.28 = (bf16[256,1024]{1,0:T(8,128)(2,1)}, bf16[256,1024]{1,0:T(8,128)(2,1)}, u32[]{:S(2)}, u32[]{:S(2)}) collective-permute-start(bf16[256,1024]{1,0:T(8,128)(2,1)} %get-tuple-element.108), channel_id=1, source_target_pairs={{2,4},{3,5},{4,6},{5,7},{10,12},{11,13},{12,14},{13,15},{18,20},{1... | collective-permute-start | bytes 1572872 | tf_op jit(solution)/shard_map/ppermute | solution.py:318
  364.1 34.7 %collective-permute-start.26 = (bf16[256,1024]{1,0:T(8,128)(2,1)}, bf16[256,1024]{1,0:T(8,128)(2,1)}, u32[]{:S(2)}, u32[]{:S(2)}) collective-permute-start(bf16[256,1024]{1,0:T(8,128)(2,1)} %get-tuple-element.121), channel_id=1, source_target_pairs={{0,4},{1,5},{6,2},{7,3},{8,12},{9,13},{14,10},{15,11},{16,20},{17,... | collective-permute-start | bytes 1572872 | tf_op jit(solution)/shard_map/ppermute | solution.py:318
  388.8 11.7 %copy-start.8 = (f32[1,256,2048]{2,1,0:T(8,128)S(1)}, f32[1,256,2048]{2,1,0:T(8,128)}, u32[]{:S(2)}) copy-start(f32[1,256,2048]{2,1,0:T(8,128)} %param.13) | copy-start | bytes 6291460
  388.9 11.7 %copy-start.10 = (f32[1,256,2048]{2,1,0:T(8,128)S(1)}, f32[1,256,2048]{2,1,0:T(8,128)}, u32[]{:S(2)}) copy-start(f32[1,256,2048]{2,1,0:T(8,128)} %param.15) | copy-start | bytes 6291460
  (8 other events, 10.7 us)
where the time goes:
time: 412 us; the launch traced here: 404 us
  waiting for transfers between devices  179 us (43%)
  Pallas kernels  81.6 us (20%)
  starting transfers between devices  71.6 us (17%)
  other arithmetic  41.9 us (10%)
  local copies, waits for them, and re-layouts  19.3 us (5%)
  matrix products  5.47 us (1%)
  between operations  4.52 us (1%)
    ppermute x34, waiting for transfers between devices, send(): return lax.ppermute(value, ('row', 'col'), pairs)  171 us
    ppermute x34, starting transfers between devices, send(): return lax.ppermute(value, ('row', 'col'), pairs)  62.9 us
    pallas_call x4, Pallas kernels, terms(): pl.pallas_call(functools.partial(term_kernel, guard * width ** 0.5, 256,...  39.2 us
    pallas_call x2, Pallas kernels, step(): pl.pallas_call(functools.partial(step_kernel, rows_dev, tile, keep, base,...  28.3 us
    pallas_call x1, Pallas kernels, update(): pl.pallas_call(functools.partial(update_kernel, guard * width ** 0.5, 512...  14.1 us
    unnamed x74, local copies, waits for them, and re-layouts  13.4 us
    sub x2, other arithmetic, outer(): module - outer_rate * (outer_moment * following + average)  11.5 us
    all_to_all x2, starting transfers between devices, exchange(): lax.all_to_all(value.reshape(paths, room, 2 * width), ('row', 'col'), spl...  8.71 us
  transfers between devices with their start and end apart: 36, of which 11 were waited for; matrix products, arithmetic and copies ran while one was open for 11% of the time, Pallas kernels for 15%

commit v1 on v0

--- a/solution.py
+++ b/solution.py
@@ -14,7 +14,7 @@
 outer_rate = 0.7
 outer_moment = 0.9
 
-STEP_VMEM = 56 * 1024 * 1024
+STEP_VMEM = 63 * 1024 * 1024
 TILE_VMEM = 32 * 1024 * 1024
 f32 = jnp.float32
 bf16 = jnp.bfloat16

time: 412 us -> 413 us (level)
    unnamed x74 -> x80, local copies, waits for them, and re-layouts: 13.4 us -> 15.5 us
  transfers between devices with their start and end apart: 36 -> 36, of which waited for: 11 -> 11; matrix products, arithmetic and copies ran while one was open for 11% -> 12% of each run, Pallas kernels for 15% -> 15%
where the time goes in v1:
time: 413 us; the launch traced here: 405 us
  waiting for transfers between devices  176 us (43%)
  Pallas kernels  82.7 us (20%)
  starting transfers between devices  71.7 us (17%)
  other arithmetic  42.3 us (10%)
  local copies, waits for them, and re-layouts  21.7 us (5%)
  matrix products  6.51 us (2%)
  between operations  4.62 us (1%)
    ppermute x34, waiting for transfers between devices, send(): return lax.ppermute(value, ('row', 'col'), pairs)  167 us
    ppermute x34, starting transfers between devices, send(): return lax.ppermute(value, ('row', 'col'), pairs)  62.8 us
    pallas_call x4, Pallas kernels, terms(): pl.pallas_call(functools.partial(term_kernel, guard * width ** 0.5, 256,...  39.2 us
    pallas_call x2, Pallas kernels, step(): pl.pallas_call(functools.partial(step_kernel, rows_dev, tile, keep, base,...  29.4 us
    unnamed x80, local copies, waits for them, and re-layouts  15.5 us
    pallas_call x1, Pallas kernels, update(): pl.pallas_call(functools.partial(update_kernel, guard * width ** 0.5, 512...  14.1 us
    sub x2, other arithmetic, outer(): module - outer_rate * (outer_moment * following + average)  11.5 us
    all_to_all x2, starting transfers between devices, exchange(): lax.all_to_all(value.reshape(paths, room, 2 * width), ('row', 'col'), spl...  8.83 us
  transfers between devices with their start and end apart: 36, of which 11 were waited for; matrix products, arithmetic and copies ran while one was open for 12% of the time, Pallas kernels for 15%

profile of v1, /device:TPU:1, one launch (start us, length us, event | category | flops | bytes accessed | tf_op | source)
XLA Modules:
  0.0 405.0 jit_solution(1561691649855212660)
XLA Ops:
  0.6 2.5 convert_bitcast_fusion
  3.1 1.5 fusion.22
  4.7 1.8 collective-permute-start.1
  6.5 5.6 %collective-permute-start = (bf16[512,1024]{1,0:T(8,128)(2,1)}, bf16[512,1024]{1,0:T(8,128)(2,1)}, u32[]{:S(2)}, u32[]{:S(2)}) collective-permute-start(bf16[512,1024]{1,0:T(8,128)(2,1)} %get-tuple-element.75), channel_id=1, source_target_pairs={{2,4},{3,5},{4,2},{5,3},{10,12},{11,13},{12,10},{13,11},{18,20},{1... | collective-permute-start | bytes 3145736 | tf_op jit(solution)/shard_map/ppermute | solution.py:318
  12.2 2.3 collective-permute-start.2
  17.3 2.4 maximum_select_fusion
  19.7 1.5 fusion.21
  21.2 1.8 collective-permute-start.5
  28.2 3.3 convolution_convert_fusion
  31.6 3.2 convolution_convert_fusion.1
  34.8 1.4 collective-permute-done
  36.1 1.3 collective-permute-start.4
  37.4 1.7 pad_maximum_fusion.refs_10_.refs_12_
  40.1 1.6 pad_maximum_fusion.1.refs_18_.refs_20_
  42.5 2.4 collective-permute-start.3
  44.9 23.3 %collective-permute-done.3 = bf16[512,1024]{1,0:T(8,128)(2,1)S(1)} collective-permute-done((bf16[512,1024]{1,0:T(8,128)(2,1)}, bf16[512,1024]{1,0:T(8,128)(2,1)S(1)}, u32[]{:S(2)}, u32[]{:S(2)}) %collective-permute-start.3) | collective-permute-done | bytes 1048608 | tf_op jit(solution)/shard_map/ppermute | solution.py:318
  68.3 18.0 %collective-permute-done.4 = bf16[512,2048]{1,0:T(8,128)(2,1)S(1)} collective-permute-done((bf16[512,2048]{1,0:T(8,128)(2,1)S(1)}, bf16[512,2048]{1,0:T(8,128)(2,1)S(1)}, u32[]{:S(2)}, u32[]{:S(2)}) %collective-permute-start.4) | collective-permute-done | bytes 2097184 | tf_op jit(solution)/shard_map/ppermute | solution.py:318
  87.7 1.9 collective-permute-start.9
  89.8 3.2 collective-permute-start.12
  92.9 3.1 collective-permute-start.11
  96.1 19.8 %collective-permute-done.9 = bf16[512,1024]{1,0:T(8,128)(2,1)S(1)} collective-permute-done((bf16[512,1024]{1,0:T(8,128)(2,1)S(1)}, bf16[512,1024]{1,0:T(8,128)(2,1)S(1)}, u32[]{:S(2)}, u32[]{:S(2)}) %collective-permute-start.9) | collective-permute-done | bytes 1048608 | tf_op jit(solution)/shard_map/ppermute | solution.py:318
  118.2 4.2 %all-to-all-start = ((bf16[32,8,4096]{2,1,0:T(8,128)(2,1)}), bf16[32,8,4096]{2,1,0:T(8,128)(2,1)}, u32[]{:S(2)}, u32[]{:S(2)}) async-start(bf16[32,8,4096]{2,1,0:T(8,128)(2,1)} %bitcast.73), calls=%async_computation | async-start | bytes 4194304 | tf_op jit(solution)/shard_map/all_to_all | solution.py:392
  122.5 3.4 collective-permute-start.14
  126.2 3.4 collective-permute-start.17
  129.6 3.1 collective-permute-start.16
  132.8 1.6 broadcast_select_fusion.2
  136.8 34.1 %collective-permute-done.14 = bf16[512,1024]{1,0:T(8,128)(2,1)S(1)} collective-permute-done((bf16[512,1024]{1,0:T(8,128)(2,1)}, bf16[512,1024]{1,0:T(8,128)(2,1)S(1)}, u32[]{:S(2)}, u32[]{:S(2)}) %collective-permute-start.14) | collective-permute-done | bytes 1048608 | tf_op jit(solution)/shard_map/ppermute | solution.py:318
  171.0 1.5 pad_maximum_fusion.3.refs_6_.refs_7_
  172.5 1.3 copy-done.38
  173.9 4.6 %all-to-all-start.1 = ((bf16[32,8,4096]{2,1,0:T(8,128)(2,1)}), bf16[32,8,4096]{2,1,0:T(8,128)(2,1)}, u32[]{:S(2)}, u32[]{:S(2)}) async-start(bf16[32,8,4096]{2,1,0:T(8,128)(2,1)} %bitcast.27), calls=%async_computation.1 | async-start | bytes 4194304 | tf_op jit(solution)/shard_map/all_to_all | solution.py:392
  178.5 16.6 %shard_map.111 = (bf16[256,4096]{1,0:T(8,128)(2,1)}, bf16[256,4096]{1,0:T(8,128)(2,1)}, bf16[4096,2048]{1,0:T(8,128)(2,1)}) custom-call(s32[84]{0:T(128)} %stack.94.refs_0_.place_ref, bf16[256,4096]{1,0:T(8,128)(2,1)} %bitcast.26.refs_1_, bf16[1024,1024]{1,0:T(8,128)(2,1)} %copy-done.18, bf16[1024,1024]{1,0:T(8,128)(2,1)} %copy-done.18, ...), custom_call_target="tpu_custom_call" | custom-call | flops 16106127360 | bytes 16777216 | tf_op jit(solution)/shard_map/pallas_call | solution.py:143
  195.1 1.6 copy-done
  196.7 1.6 copy-done.2
  198.3 14.1 %shard_map.112.refs_2_.refs_3_ = bf16[4096,2048]{1,0:T(8,128)(2,1)S(1)} custom-call(bf16[256,4096]{1,0:T(8,128)(2,1)S(1)} %copy-done, bf16[256,4096]{1,0:T(8,128)(2,1)S(1)} %copy-done.2, bf16[4096,2048]{1,0:T(8,128)(2,1)} %get-tuple-element.93.p_ref), custom_call_target="tpu_custom_call" | custom-call | flops 25769803776 | bytes 33554432 | tf_op jit(solution)/shard_map/pallas_call | solution.py:177
  212.4 5.8 %copy-done.5 = bf16[4096,2048]{1,0:T(8,128)(2,1)} copy-done((bf16[4096,2048]{1,0:T(8,128)(2,1)}, bf16[4096,2048]{1,0:T(8,128)(2,1)S(1)}, u32[]{:S(2)}) %copy-start.5) | copy-done | bytes 16777240
  218.2 8.4 %all-to-all-done.1 = bf16[32,8,4096]{2,1,0:T(8,128)(2,1)} async-done(((bf16[32,8,4096]{2,1,0:T(8,128)(2,1)}), bf16[32,8,4096]{2,1,0:T(8,128)(2,1)}, u32[]{:S(2)}, u32[]{:S(2)}) %all-to-all-start.1) | async-done | bytes 2097184 | tf_op jit(solution)/shard_map/all_to_all | solution.py:392
  226.6 12.9 %shard_map.113 = (bf16[256,4096]{1,0:T(8,128)(2,1)S(1)}, bf16[256,4096]{1,0:T(8,128)(2,1)S(1)}) custom-call(s32[84]{0:T(128)S(1)} %copy-done.4, bf16[256,4096]{1,0:T(8,128)(2,1)} %bitcast.28.refs_1_, bf16[4096,2048]{1,0:T(8,128)(2,1)} %copy-done.5, bf16[4096,2048]{1,0:T(8,128)(2,1)} %copy-done.5), custom_call_target="tpu_custom_call" | custom-call | flops 16106127360 | bytes 16777216 | tf_op jit(solution)/shard_map/pallas_call | solution.py:143
  239.5 9.7 %shard_map.114 = (bf16[1024,1024]{1,0:T(8,128)(2,1)S(1)}, bf16[1024,1024]{1,0:T(8,128)(2,1)S(1)}) custom-call(s32[84]{0:T(128)S(1)} %copy-done.4, f32[2]{0:T(128)S(1)} %pad_maximum_fusion.4.weight_ref, bf16[256,4096]{1,0:T(8,128)(2,1)S(1)} %copy-done.1, bf16[256,4096]{1,0:T(8,128)(2,1)S(1)} %copy-done.3, bf16[256,4096]{1,0:T(8,128)(2,1)S(1)} %get-tuple-element.94.c_ref, ...), custom_call_target="tpu_custom_call" | custom-call | flops 1 | bytes 1 | tf_op jit(solution)/shard_map/pallas_call | solution.py:256
  249.8 9.7 %shard_map.115 = (bf16[1024,1024]{1,0:T(8,128)(2,1)S(1)}, bf16[1024,1024]{1,0:T(8,128)(2,1)S(1)}) custom-call(s32[84]{0:T(128)S(1)} %copy-done.4, f32[2]{0:T(128)S(1)} %pad_maximum_fusion.4.weight_ref, bf16[256,4096]{1,0:T(8,128)(2,1)S(1)} %copy-done.1, bf16[256,4096]{1,0:T(8,128)(2,1)S(1)} %copy-done.3, bf16[256,4096]{1,0:T(8,128)(2,1)S(1)} %get-tuple-element.94.c_ref, ...), custom_call_target="tpu_custom_call" | custom-call | flops 1 | bytes 1 | tf_op jit(solution)/shard_map/pallas_call | solution.py:256
  260.0 2.0 collective-permute-start.19
  262.0 1.4 add_convert_fusion.2
  263.4 10.0 %shard_map.116 = (bf16[1024,1024]{1,0:T(8,128)(2,1)S(1)}, bf16[1024,1024]{1,0:T(8,128)(2,1)S(1)}) custom-call(s32[84]{0:T(128)S(1)} %copy-done.4, f32[2]{0:T(128)S(1)} %pad_maximum_fusion.4.weight_ref, bf16[256,4096]{1,0:T(8,128)(2,1)S(1)} %copy-done.1, bf16[256,4096]{1,0:T(8,128)(2,1)S(1)} %copy-done.3, bf16[256,4096]{1,0:T(8,128)(2,1)S(1)} %get-tuple-element.94.c_ref, ...), custom_call_target="tpu_custom_call" | custom-call | flops 1 | bytes 1 | tf_op jit(solution)/shard_map/pallas_call | solution.py:256
  275.1 10.0 %collective-permute-done.19 = bf16[512,1024]{1,0:T(8,128)(2,1)S(1)} collective-permute-done((bf16[512,1024]{1,0:T(8,128)(2,1)S(1)}, bf16[512,1024]{1,0:T(8,128)(2,1)S(1)}, u32[]{:S(2)}, u32[]{:S(2)}) %collective-permute-start.19) | collective-permute-done | bytes 1048608 | tf_op jit(solution)/shard_map/ppermute | solution.py:318
  285.1 1.6 fusion
  286.7 4.1 %collective-permute-start.20 = (bf16[512,1024]{1,0:T(8,128)(2,1)}, bf16[512,1024]{1,0:T(8,128)(2,1)}, u32[]{:S(2)}, u32[]{:S(2)}) collective-permute-start(bf16[512,1024]{1,0:T(8,128)(2,1)} %fusion), channel_id=1, source_target_pairs={{2,4},{3,5},{4,2},{5,3},{10,12},{11,13},{12,10},{13,11},{18,20},{1... | collective-permute-start | bytes 3145736 | tf_op jit(solution)/shard_map/ppermute | solution.py:318
  290.8 9.7 %shard_map.117 = (bf16[1024,1024]{1,0:T(8,128)(2,1)S(1)}, bf16[1024,1024]{1,0:T(8,128)(2,1)S(1)}) custom-call(s32[84]{0:T(128)S(1)} %copy-done.4, f32[2]{0:T(128)S(1)} %pad_maximum_fusion.4.weight_ref, bf16[256,4096]{1,0:T(8,128)(2,1)S(1)} %copy-done.1, bf16[256,4096]{1,0:T(8,128)(2,1)S(1)} %copy-done.3, bf16[256,4096]{1,0:T(8,128)(2,1)S(1)} %get-tuple-element.94.c_ref, ...), custom_call_target="tpu_custom_call" | custom-call | flops 1 | bytes 1 | tf_op jit(solution)/shard_map/pallas_call | solution.py:256
  300.6 18.2 %collective-permute-done.22 = bf16[512,1024]{1,0:T(8,128)(2,1)S(1)} collective-permute-done((bf16[512,1024]{1,0:T(8,128)(2,1)}, bf16[512,1024]{1,0:T(8,128)(2,1)S(1)}, u32[]{:S(2)}, u32[]{:S(2)}) %collective-permute-start.22) | collective-permute-done | bytes 1048608 | tf_op jit(solution)/shard_map/ppermute | solution.py:318
  319.5 1.9 collective-permute-start.23
  321.9 1.6 collective-permute-start.30
  324.2 3.4 convert_select_fusion.1
  327.6 19.3 %collective-permute-done.23 = bf16[512,1024]{1,0:T(8,128)(2,1)S(1)} collective-permute-done((bf16[512,1024]{1,0:T(8,128)(2,1)S(1)}, bf16[512,1024]{1,0:T(8,128)(2,1)S(1)}, u32[]{:S(2)}, u32[]{:S(2)}) %collective-permute-start.23) | collective-permute-done | bytes 1048608 | tf_op jit(solution)/shard_map/ppermute | solution.py:318
  346.9 2.2 convert_select_fusion
  350.8 1.8 collective-permute-start.32
  352.6 1.9 collective-permute-start.33
  354.5 1.3 collective-permute-start.31
  357.7 5.4 %collective-permute-start.27 = (bf16[256,1024]{1,0:T(8,128)(2,1)}, bf16[256,1024]{1,0:T(8,128)(2,1)}, u32[]{:S(2)}, u32[]{:S(2)}) collective-permute-start(bf16[256,1024]{1,0:T(8,128)(2,1)} %get-tuple-element.107), channel_id=1, source_target_pairs={{2,0},{3,1},{4,2},{5,3},{10,8},{11,9},{12,10},{13,11},{18,16},{19,... | collective-permute-start | bytes 1572872 | tf_op jit(solution)/shard_map/ppermute | solution.py:318
  363.0 2.2 collective-permute-start.28
  365.2 1.6 collective-permute-start.26
  366.8 8.8 %multiply_subtract_fusion = (f32[1,512,2048]{2,1,0:T(8,128)}, f32[1,512,2048]{2,1,0:T(8,128)}) fusion(f32[1,512,2048]{2,1,0:T(8,128)S(1)} %copy-done.6, f32[512,1024]{1,0:T(8,128)} %convert_select_fusion, f32[512,1024]{1,0:T(8,128)} %convert_select_fusion.1, f32[1,512,2048]{2,1,0:T(8,128)} %param.14), kind=kLoop, calls=%fused_computation.3 | loop fusion | flops 7340032 | bytes 20971520 | tf_op jit(solution)/shard_map/sub | solution.py:520
  375.6 13.1 %collective-permute-done.33 = bf16[256,1024]{1,0:T(8,128)(2,1)S(1)} collective-permute-done((bf16[256,1024]{1,0:T(8,128)(2,1)}, bf16[256,1024]{1,0:T(8,128)(2,1)S(1)}, u32[]{:S(2)}, u32[]{:S(2)}) %collective-permute-start.33) | collective-permute-done | bytes 524320 | tf_op jit(solution)/shard_map/ppermute | solution.py:318
  388.7 1.4 select_add_fusion
  390.2 9.9 %collective-permute-done.28 = bf16[256,1024]{1,0:T(8,128)(2,1)} collective-permute-done((bf16[256,1024]{1,0:T(8,128)(2,1)}, bf16[256,1024]{1,0:T(8,128)(2,1)}, u32[]{:S(2)}, u32[]{:S(2)}) %collective-permute-start.28) | collective-permute-done | bytes 524320 | tf_op jit(solution)/shard_map/ppermute | solution.py:318
  400.0 1.8 select_add_fusion.1
  401.8 2.7 multiply_subtract_fusion.1
  (150 shorter events, 22.1 us)
Async XLA Ops:
  3.1 8.9 %copy-start.7 = (f32[1,256,2048]{2,1,0:T(8,128)S(1)}, f32[1,256,2048]{2,1,0:T(8,128)}, u32[]{:S(2)}) copy-start(f32[1,256,2048]{2,1,0:T(8,128)} %param.13) | copy-start | bytes 6291460
  4.7 9.9 %copy-start.35 = (s32[2,128,1]{1,2,0:T(1,128)S(1)}, s32[2,128,1]{1,2,0:T(1,128)}, u32[]{:S(2)}) copy-start(s32[2,128,1]{1,2,0:T(1,128)} %param.10) | copy-start | bytes 3076
  4.7 10.5 %copy-start.22 = (bf16[2,128,2048]{2,1,0:T(8,128)(2,1)S(1)}, bf16[2,128,2048]{2,1,0:T(8,128)(2,1)}, u32[]{:S(2)}) copy-start(bf16[2,128,2048]{2,1,0:T(8,128)(2,1)} %param.8) | copy-start | bytes 3145732
  4.7 11.6 %copy-start.23 = (bf16[2,128,2048]{2,1,0:T(8,128)(2,1)S(1)}, bf16[2,128,2048]{2,1,0:T(8,128)(2,1)}, u32[]{:S(2)}) copy-start(bf16[2,128,2048]{2,1,0:T(8,128)(2,1)} %param.9) | copy-start | bytes 3145732
  4.7 30.1 %collective-permute-start.1 = (bf16[512,1024]{1,0:T(8,128)(2,1)}, bf16[512,1024]{1,0:T(8,128)(2,1)}, u32[]{:S(2)}, u32[]{:S(2)}) collective-permute-start(bf16[512,1024]{1,0:T(8,128)(2,1)} %get-tuple-element.75), channel_id=1, source_target_pairs={{0,1},{1,0},{6,7},{7,6},{8,9},{9,8},{14,15},{15,14},{16,17},{17,16... | collective-permute-start | bytes 3145736 | tf_op jit(solution)/shard_map/ppermute | solution.py:318
  6.5 29.7 %collective-permute-start = (bf16[512,1024]{1,0:T(8,128)(2,1)}, bf16[512,1024]{1,0:T(8,128)(2,1)}, u32[]{:S(2)}, u32[]{:S(2)}) collective-permute-start(bf16[512,1024]{1,0:T(8,128)(2,1)} %get-tuple-element.75), channel_id=1, source_target_pairs={{2,4},{3,5},{4,2},{5,3},{10,12},{11,13},{12,10},{13,11},{18,20},{1... | collective-permute-start | bytes 3145736 | tf_op jit(solution)/shard_map/ppermute | solution.py:318
  12.2 5.1 %collective-permute-start.2 = (bf16[256,2048]{1,0:T(8,128)(2,1)S(1)}, bf16[256,2048]{1,0:T(8,128)(2,1)}, u32[]{:S(2)}, u32[]{:S(2)}) collective-permute-start(bf16[256,2048]{1,0:T(8,128)(2,1)S(1)} %convert_bitcast_fusion.1), channel_id=1, source_target_pairs={{2,6},{3,7},{4,0},{5,1},{10,14},{11,15},{12,8},{13,9},{18,22},{19,... | collective-permute-start | bytes 3145736 | tf_op jit(solution)/shard_map/ppermute | solution.py:318
  19.7 3.3 copy-start.34
  21.2 10.3 %copy-start.19 = (bf16[128,2048]{1,0:T(8,128)(2,1)S(1)}, bf16[128,2048]{1,0:T(8,128)(2,1)}, u32[]{:S(2)}) copy-start(bf16[128,2048]{1,0:T(8,128)(2,1)} %get-tuple-element.134) | copy-start | bytes 1572868
  21.2 16.2 %collective-permute-start.5 = (bf16[512,1024]{1,0:T(8,128)(2,1)}, bf16[512,1024]{1,0:T(8,128)(2,1)}, u32[]{:S(2)}, u32[]{:S(2)}) collective-permute-start(bf16[512,1024]{1,0:T(8,128)(2,1)} %get-tuple-element.130), channel_id=1, source_target_pairs={{0,8},{1,9},{6,14},{7,15},{8,0},{9,1},{14,6},{15,7},{16,24},{17,25... | collective-permute-start | bytes 3145736 | tf_op jit(solution)/shard_map/ppermute | solution.py:318
  27.4 12.7 %collective-permute-start.7 = (bf16[512,1024]{1,0:T(8,128)(2,1)}, bf16[512,1024]{1,0:T(8,128)(2,1)S(1)}, u32[]{:S(2)}, u32[]{:S(2)}) collective-permute-start(bf16[512,1024]{1,0:T(8,128)(2,1)} %get-tuple-element.129), channel_id=1, source_target_pairs={{0,16},{1,17},{6,22},{7,23},{8,24},{9,25},{14,30},{15,31},{16,0},{... | collective-permute-start | bytes 3145736 | tf_op jit(solution)/shard_map/ppermute | solution.py:318
  36.1 50.1 %collective-permute-start.4 = (bf16[512,2048]{1,0:T(8,128)(2,1)S(1)}, bf16[512,2048]{1,0:T(8,128)(2,1)S(1)}, u32[]{:S(2)}, u32[]{:S(2)}) collective-permute-start(bf16[512,2048]{1,0:T(8,128)(2,1)S(1)} %maximum_select_fusion), channel_id=1, source_target_pairs={{0,2},{1,3},{6,4},{7,5},{8,10},{9,11},{14,12},{15,13},{16,18},{17,... | collective-permute-start | bytes 6291464 | tf_op jit(solution)/shard_map/ppermute | solution.py:318
  39.2 47.1 %copy-start.9 = (bf16[512,1024]{1,0:T(8,128)(2,1)S(1)}, bf16[512,1024]{1,0:T(8,128)(2,1)}, u32[]{:S(2)}) copy-start(bf16[512,1024]{1,0:T(8,128)(2,1)} %get-tuple-element.69) | copy-start | bytes 3145732
  39.2 47.1 %collective-permute-start.6 = (bf16[1024,1024]{1,0:T(8,128)(2,1)S(1)}, bf16[1024,1024]{1,0:T(8,128)(2,1)S(1)}, u32[]{:S(2)}, u32[]{:S(2)}) collective-permute-start(bf16[1024,1024]{1,0:T(8,128)(2,1)S(1)} %pad_maximum_fusion.refs_10_.refs_12_), channel_id=1, source_target_pairs={{0,16},{1,17},{6,22},{7,23},{8,24},{9,25},{14,30},{15,31},{16,0},{... | collective-permute-start | bytes 6291464 | tf_op jit(solution)/shard_map/ppermute | solution.py:318
  41.7 48.0 %copy-start.17 = (bf16[1024,1024]{1,0:T(8,128)(2,1)}, bf16[1024,1024]{1,0:T(8,128)(2,1)S(1)}, u32[]{:S(2)}) copy-start(bf16[1024,1024]{1,0:T(8,128)(2,1)S(1)} %pad_maximum_fusion.1.refs_18_.refs_20_) | copy-start | bytes 6291460
  41.7 44.5 %collective-permute-start.8 = (bf16[1024,1024]{1,0:T(8,128)(2,1)S(1)}, bf16[1024,1024]{1,0:T(8,128)(2,1)S(1)}, u32[]{:S(2)}, u32[]{:S(2)}) collective-permute-start(bf16[1024,1024]{1,0:T(8,128)(2,1)S(1)} %pad_maximum_fusion.1.refs_18_.refs_20_), channel_id=1, source_target_pairs={{0,8},{1,9},{6,14},{7,15},{8,0},{9,1},{14,6},{15,7},{16,24},{17,25... | collective-permute-start | bytes 6291464 | tf_op jit(solution)/shard_map/ppermute | solution.py:318
  42.5 25.7 %collective-permute-start.3 = (bf16[512,1024]{1,0:T(8,128)(2,1)}, bf16[512,1024]{1,0:T(8,128)(2,1)S(1)}, u32[]{:S(2)}, u32[]{:S(2)}) collective-permute-start(bf16[512,1024]{1,0:T(8,128)(2,1)} %collective-permute-done), channel_id=1, source_target_pairs={{2,3},{3,2},{4,5},{5,4},{10,11},{11,10},{12,13},{13,12},{18,19},{1... | collective-permute-start | bytes 3145736 | tf_op jit(solution)/shard_map/ppermute | solution.py:318
  68.3 18.7 %copy-start.20 = (bf16[512,1024]{1,0:T(8,128)(2,1)}, bf16[512,1024]{1,0:T(8,128)(2,1)S(1)}, u32[]{:S(2)}) copy-start(bf16[512,1024]{1,0:T(8,128)(2,1)S(1)} %collective-permute-done.3) | copy-start | bytes 3145732
  86.3 3.5 copy-start.36
  86.3 9.8 %collective-permute-start.10 = (bf16[512,1024]{1,0:T(8,128)(2,1)S(1)}, bf16[512,1024]{1,0:T(8,128)(2,1)S(1)}, u32[]{:S(2)}, u32[]{:S(2)}) collective-permute-start(bf16[512,1024]{1,0:T(8,128)(2,1)S(1)} %copy-done.9), channel_id=1, source_target_pairs={{0,1},{1,0},{6,7},{7,6},{8,9},{9,8},{14,15},{15,14},{16,17},{17,16... | collective-permute-start | bytes 3145736 | tf_op jit(solution)/shard_map/ppermute | solution.py:318
  87.7 28.2 %collective-permute-start.9 = (bf16[512,1024]{1,0:T(8,128)(2,1)S(1)}, bf16[512,1024]{1,0:T(8,128)(2,1)S(1)}, u32[]{:S(2)}, u32[]{:S(2)}) collective-permute-start(bf16[512,1024]{1,0:T(8,128)(2,1)S(1)} %copy-done.9), channel_id=1, source_target_pairs={{2,4},{3,5},{4,2},{5,3},{10,12},{11,13},{12,10},{13,11},{18,20},{1... | collective-permute-start | bytes 3145736 | tf_op jit(solution)/shard_map/ppermute | solution.py:318
  89.8 26.1 %collective-permute-start.12 = (bf16[512,1024]{1,0:T(8,128)(2,1)S(1)}, bf16[512,1024]{1,0:T(8,128)(2,1)S(1)}, u32[]{:S(2)}, u32[]{:S(2)}) collective-permute-start(bf16[512,1024]{1,0:T(8,128)(2,1)S(1)} %get-tuple-element.86), channel_id=1, source_target_pairs={{2,18},{3,19},{4,20},{5,21},{10,26},{11,27},{12,28},{13,29},{18,2}... | collective-permute-start | bytes 3145736 | tf_op jit(solution)/shard_map/ppermute | solution.py:318
  92.9 23.0 %collective-permute-start.11 = (bf16[512,1024]{1,0:T(8,128)(2,1)S(1)}, bf16[512,1024]{1,0:T(8,128)(2,1)S(1)}, u32[]{:S(2)}, u32[]{:S(2)}) collective-permute-start(bf16[512,1024]{1,0:T(8,128)(2,1)S(1)} %get-tuple-element.82), channel_id=1, source_target_pairs={{2,10},{3,11},{4,12},{5,13},{10,2},{11,3},{12,4},{13,5},{18,26},{1... | collective-permute-start | bytes 3145736 | tf_op jit(solution)/shard_map/ppermute | solution.py:318
  96.1 19.8 %copy-start.24 = (bf16[512,1024]{1,0:T(8,128)(2,1)}, bf16[512,1024]{1,0:T(8,128)(2,1)S(1)}, u32[]{:S(2)}) copy-start(bf16[512,1024]{1,0:T(8,128)(2,1)S(1)} %collective-permute-done.10) | copy-start | bytes 3145732
  118.2 55.6 %all-to-all-start = ((bf16[32,8,4096]{2,1,0:T(8,128)(2,1)}), bf16[32,8,4096]{2,1,0:T(8,128)(2,1)}, u32[]{:S(2)}, u32[]{:S(2)}) async-start(bf16[32,8,4096]{2,1,0:T(8,128)(2,1)} %bitcast.73), calls=%async_computation | async-start | bytes 4194304 | tf_op jit(solution)/shard_map/all_to_all | solution.py:392
  122.5 3.6 copy-start.31
  122.5 48.4 %collective-permute-start.14 = (bf16[512,1024]{1,0:T(8,128)(2,1)}, bf16[512,1024]{1,0:T(8,128)(2,1)S(1)}, u32[]{:S(2)}, u32[]{:S(2)}) collective-permute-start(bf16[512,1024]{1,0:T(8,128)(2,1)} %copy-done.26), channel_id=1, source_target_pairs={{2,3},{3,2},{4,5},{5,4},{10,11},{11,10},{12,13},{13,12},{18,19},{1... | collective-permute-start | bytes 3145736 | tf_op jit(solution)/shard_map/ppermute | solution.py:318
  126.0 3.6 copy-start.29
  126.1 6.7 %copy-start.21 = (bf16[512,1024]{1,0:T(8,128)(2,1)S(1)}, bf16[512,1024]{1,0:T(8,128)(2,1)}, u32[]{:S(2)}) copy-start(bf16[512,1024]{1,0:T(8,128)(2,1)} %copy-done.20) | copy-start | bytes 3145732
  126.2 8.2 %copy-start.33 = (bf16[1024,1024]{1,0:T(8,128)(2,1)}, bf16[1024,1024]{1,0:T(8,128)(2,1)S(1)}, u32[]{:S(2)}) copy-start(bf16[1024,1024]{1,0:T(8,128)(2,1)S(1)} %constant_dynamic-update-slice_fusion.2.refs_19_.refs_21_) | copy-start | bytes 6291460
  126.2 46.4 %collective-permute-start.17 = (bf16[1024,1024]{1,0:T(8,128)(2,1)S(1)}, bf16[1024,1024]{1,0:T(8,128)(2,1)S(1)}, u32[]{:S(2)}, u32[]{:S(2)}) collective-permute-start(bf16[1024,1024]{1,0:T(8,128)(2,1)S(1)} %constant_dynamic-update-slice_fusion.2.refs_19_.refs_21_), channel_id=1, source_target_pairs={{2,10},{3,11},{4,12},{5,13},{10,2},{11,3},{12,4},{13,5},{18,26},{1... | collective-permute-start | bytes 6291464 | tf_op jit(solution)/shard_map/ppermute | solution.py:318
  129.6 4.7 %copy-start.32 = (bf16[1024,1024]{1,0:T(8,128)(2,1)}, bf16[1024,1024]{1,0:T(8,128)(2,1)S(1)}, u32[]{:S(2)}) copy-start(bf16[1024,1024]{1,0:T(8,128)(2,1)S(1)} %constant_dynamic-update-slice_fusion.refs_11_.refs_13_) | copy-start | bytes 6291460
  129.6 44.2 %collective-permute-start.16 = (bf16[1024,1024]{1,0:T(8,128)(2,1)S(1)}, bf16[1024,1024]{1,0:T(8,128)(2,1)}, u32[]{:S(2)}, u32[]{:S(2)}) collective-permute-start(bf16[1024,1024]{1,0:T(8,128)(2,1)S(1)} %constant_dynamic-update-slice_fusion.refs_11_.refs_13_), channel_id=1, source_target_pairs={{2,18},{3,19},{4,20},{5,21},{10,26},{11,27},{12,28},{13,29},{18,2}... | collective-permute-start | bytes 6291464 | tf_op jit(solution)/shard_map/ppermute | solution.py:318
  134.6 36.5 %copy-start.18 = (bf16[1024,1024]{1,0:T(8,128)(2,1)}, bf16[1024,1024]{1,0:T(8,128)(2,1)S(1)}, u32[]{:S(2)}) copy-start(bf16[1024,1024]{1,0:T(8,128)(2,1)S(1)} %pad_maximum_fusion.2.refs_2_.refs_3_) | copy-start | bytes 6291460
  134.6 36.3 %copy-start.25 = (bf16[512,1024]{1,0:T(8,128)(2,1)S(1)}, bf16[512,1024]{1,0:T(8,128)(2,1)}, u32[]{:S(2)}) copy-start(bf16[512,1024]{1,0:T(8,128)(2,1)} %copy-done.24) | copy-start | bytes 3145732
  134.6 43.9 %collective-permute-start.13 = (bf16[1024,1024]{1,0:T(8,128)(2,1)S(1)}, bf16[1024,1024]{1,0:T(8,128)(2,1)}, u32[]{:S(2)}, u32[]{:S(2)}) collective-permute-start(bf16[1024,1024]{1,0:T(8,128)(2,1)S(1)} %pad_maximum_fusion.2.refs_2_.refs_3_), channel_id=1, source_target_pairs={{0,4},{1,5},{2,6},{3,7},{4,0},{5,1},{6,2},{7,3},{8,12},{9,13},{10,... | collective-permute-start | bytes 6291464 | tf_op jit(solution)/shard_map/ppermute | solution.py:318
  172.5 6.0 %collective-permute-start.15 = (bf16[1024,1024]{1,0:T(8,128)(2,1)}, bf16[1024,1024]{1,0:T(8,128)(2,1)}, u32[]{:S(2)}, u32[]{:S(2)}) collective-permute-start(bf16[1024,1024]{1,0:T(8,128)(2,1)} %pad_maximum_fusion.3.refs_6_.refs_7_), channel_id=1, source_target_pairs={{0,4},{1,5},{2,6},{3,7},{4,0},{5,1},{6,2},{7,3},{8,12},{9,13},{10,... | collective-permute-start | bytes 6291464 | tf_op jit(solution)/shard_map/ppermute | solution.py:318
  173.9 52.7 %all-to-all-start.1 = ((bf16[32,8,4096]{2,1,0:T(8,128)(2,1)}), bf16[32,8,4096]{2,1,0:T(8,128)(2,1)}, u32[]{:S(2)}, u32[]{:S(2)}) async-start(bf16[32,8,4096]{2,1,0:T(8,128)(2,1)} %bitcast.27), calls=%async_computation.1 | async-start | bytes 4194304 | tf_op jit(solution)/shard_map/all_to_all | solution.py:392
  198.3 28.3 %copy-start.4 = (s32[84]{0:T(128)S(1)}, s32[84]{0:T(128)}, u32[]{:S(2)}) copy-start(s32[84]{0:T(128)} %stack.94.refs_0_.place_ref) | copy-start | bytes 1012
  212.4 5.8 %copy-start.5 = (bf16[4096,2048]{1,0:T(8,128)(2,1)}, bf16[4096,2048]{1,0:T(8,128)(2,1)S(1)}, u32[]{:S(2)}) copy-start(bf16[4096,2048]{1,0:T(8,128)(2,1)S(1)} %shard_map.112.refs_2_.refs_3_) | copy-start | bytes 50331652
  226.6 12.9 %copy-start.1 = (bf16[256,4096]{1,0:T(8,128)(2,1)S(1)}, bf16[256,4096]{1,0:T(8,128)(2,1)}, u32[]{:S(2)}) copy-start(bf16[256,4096]{1,0:T(8,128)(2,1)} %get-tuple-element.89.a_ref) | copy-start | bytes 6291460
  226.6 12.9 %copy-start.3 = (bf16[256,4096]{1,0:T(8,128)(2,1)S(1)}, bf16[256,4096]{1,0:T(8,128)(2,1)}, u32[]{:S(2)}) copy-start(bf16[256,4096]{1,0:T(8,128)(2,1)} %get-tuple-element.90.b_ref) | copy-start | bytes 6291460
  249.2 10.3 %collective-permute-start.18 = (bf16[1024,1024]{1,0:T(8,128)(2,1)S(1)}, bf16[1024,1024]{1,0:T(8,128)(2,1)S(1)}, u32[]{:S(2)}, u32[]{:S(2)}) collective-permute-start(bf16[1024,1024]{1,0:T(8,128)(2,1)S(1)} %get-tuple-element.96), channel_id=1, source_target_pairs={{0,4},{1,5},{2,6},{3,7},{4,0},{5,1},{6,2},{7,3},{8,12},{9,13},{10,... | collective-permute-start | bytes 6291464 | tf_op jit(solution)/shard_map/ppermute | solution.py:318
  249.3 12.7 %collective-permute-start.21 = (bf16[1024,1024]{1,0:T(8,128)(2,1)S(1)}, bf16[1024,1024]{1,0:T(8,128)(2,1)S(1)}, u32[]{:S(2)}, u32[]{:S(2)}) collective-permute-start(bf16[1024,1024]{1,0:T(8,128)(2,1)S(1)} %get-tuple-element.100), channel_id=1, source_target_pairs={{0,4},{1,5},{2,6},{3,7},{4,0},{5,1},{6,2},{7,3},{8,12},{9,13},{10,... | collective-permute-start | bytes 6291464 | tf_op jit(solution)/shard_map/ppermute | solution.py:318
  260.0 25.1 %collective-permute-start.19 = (bf16[512,1024]{1,0:T(8,128)(2,1)S(1)}, bf16[512,1024]{1,0:T(8,128)(2,1)S(1)}, u32[]{:S(2)}, u32[]{:S(2)}) collective-permute-start(bf16[512,1024]{1,0:T(8,128)(2,1)S(1)} %add_convert_fusion.3), channel_id=1, source_target_pairs={{0,1},{1,0},{2,3},{3,2},{4,5},{5,4},{6,7},{7,6},{8,9},{9,8},{10,11... | collective-permute-start | bytes 3145736 | tf_op jit(solution)/shard_map/ppermute | solution.py:318
  273.3 48.1 %collective-permute-start.29 = (bf16[1024,1024]{1,0:T(8,128)(2,1)S(1)}, bf16[1024,1024]{1,0:T(8,128)(2,1)S(1)}, u32[]{:S(2)}, u32[]{:S(2)}) collective-permute-start(bf16[1024,1024]{1,0:T(8,128)(2,1)S(1)} %get-tuple-element.110), channel_id=1, source_target_pairs={{0,16},{1,17},{2,18},{3,19},{4,20},{5,21},{6,22},{7,23},{8,24},{9,... | collective-permute-start | bytes 6291464 | tf_op jit(solution)/shard_map/ppermute | solution.py:318
  273.7 49.8 %collective-permute-start.24 = (bf16[1024,1024]{1,0:T(8,128)(2,1)S(1)}, bf16[1024,1024]{1,0:T(8,128)(2,1)S(1)}, u32[]{:S(2)}, u32[]{:S(2)}) collective-permute-start(bf16[1024,1024]{1,0:T(8,128)(2,1)S(1)} %get-tuple-element.102), channel_id=1, source_target_pairs={{0,8},{1,9},{2,10},{3,11},{4,12},{5,13},{6,14},{7,15},{8,0},{9,1},... | collective-permute-start | bytes 6291464 | tf_op jit(solution)/shard_map/ppermute | solution.py:318
  274.7 44.2 %collective-permute-start.22 = (bf16[512,1024]{1,0:T(8,128)(2,1)}, bf16[512,1024]{1,0:T(8,128)(2,1)S(1)}, u32[]{:S(2)}, u32[]{:S(2)}) collective-permute-start(bf16[512,1024]{1,0:T(8,128)(2,1)} %add_convert_fusion.2), channel_id=1, source_target_pairs={{0,1},{1,0},{2,3},{3,2},{4,5},{5,4},{6,7},{7,6},{8,9},{9,8},{10,11... | collective-permute-start | bytes 3145736 | tf_op jit(solution)/shard_map/ppermute | solution.py:318
  286.7 35.1 %collective-permute-start.20 = (bf16[512,1024]{1,0:T(8,128)(2,1)}, bf16[512,1024]{1,0:T(8,128)(2,1)}, u32[]{:S(2)}, u32[]{:S(2)}) collective-permute-start(bf16[512,1024]{1,0:T(8,128)(2,1)} %fusion), channel_id=1, source_target_pairs={{2,4},{3,5},{4,2},{5,3},{10,12},{11,13},{12,10},{13,11},{18,20},{1... | collective-permute-start | bytes 3145736 | tf_op jit(solution)/shard_map/ppermute | solution.py:318
  319.5 27.4 %collective-permute-start.23 = (bf16[512,1024]{1,0:T(8,128)(2,1)S(1)}, bf16[512,1024]{1,0:T(8,128)(2,1)S(1)}, u32[]{:S(2)}, u32[]{:S(2)}) collective-permute-start(bf16[512,1024]{1,0:T(8,128)(2,1)S(1)} %fusion.1), channel_id=1, source_target_pairs={{2,4},{3,5},{4,2},{5,3},{10,12},{11,13},{12,10},{13,11},{18,20},{1... | collective-permute-start | bytes 3145736 | tf_op jit(solution)/shard_map/ppermute | solution.py:318
  321.9 27.2 %collective-permute-start.30 = (bf16[512,1024]{1,0:T(8,128)(2,1)S(1)}, bf16[512,1024]{1,0:T(8,128)(2,1)S(1)}, u32[]{:S(2)}, u32[]{:S(2)}) collective-permute-start(bf16[512,1024]{1,0:T(8,128)(2,1)S(1)} %add_convert_fusion), channel_id=1, source_target_pairs={{0,8},{1,9},{2,10},{3,11},{4,12},{5,13},{6,14},{7,15},{8,0},{9,1},... | collective-permute-start | bytes 3145736 | tf_op jit(solution)/shard_map/ppermute | solution.py:318
  323.5 4.1 %copy-start.12 = (bf16[1024,1024]{1,0:T(8,128)(2,1)}, bf16[1024,1024]{1,0:T(8,128)(2,1)S(1)}, u32[]{:S(2)}) copy-start(bf16[1024,1024]{1,0:T(8,128)(2,1)S(1)} %collective-permute-done.24) | copy-start | bytes 6291460
  323.9 31.9 %collective-permute-start.25 = (bf16[512,1024]{1,0:T(8,128)(2,1)S(1)}, bf16[512,1024]{1,0:T(8,128)(2,1)S(1)}, u32[]{:S(2)}, u32[]{:S(2)}) collective-permute-start(bf16[512,1024]{1,0:T(8,128)(2,1)S(1)} %add_convert_fusion.1), channel_id=1, source_target_pairs={{0,16},{1,17},{2,18},{3,19},{4,20},{5,21},{6,22},{7,23},{8,24},{9,... | collective-permute-start | bytes 3145736 | tf_op jit(solution)/shard_map/ppermute | solution.py:318
  327.6 21.5 %copy-start.15 = (bf16[1024,1024]{1,0:T(8,128)(2,1)S(1)}, bf16[1024,1024]{1,0:T(8,128)(2,1)}, u32[]{:S(2)}) copy-start(bf16[1024,1024]{1,0:T(8,128)(2,1)} %copy-done.14) | copy-start | bytes 6291460
  349.7 6.2 %copy-start.13 = (bf16[1024,1024]{1,0:T(8,128)(2,1)S(1)}, bf16[1024,1024]{1,0:T(8,128)(2,1)}, u32[]{:S(2)}) copy-start(bf16[1024,1024]{1,0:T(8,128)(2,1)} %copy-done.12) | copy-start | bytes 6291460
  350.8 14.4 %collective-permute-start.32 = (bf16[256,1024]{1,0:T(8,128)(2,1)S(1)}, bf16[256,1024]{1,0:T(8,128)(2,1)S(1)}, u32[]{:S(2)}, u32[]{:S(2)}) collective-permute-start(bf16[256,1024]{1,0:T(8,128)(2,1)S(1)} %get-tuple-element.112), channel_id=1, source_target_pairs={{2,0},{3,1},{4,2},{5,3},{10,8},{11,9},{12,10},{13,11},{18,16},{19,... | collective-permute-start | bytes 1572872 | tf_op jit(solution)/shard_map/ppermute | solution.py:318
  352.6 36.1 %collective-permute-start.33 = (bf16[256,1024]{1,0:T(8,128)(2,1)}, bf16[256,1024]{1,0:T(8,128)(2,1)S(1)}, u32[]{:S(2)}, u32[]{:S(2)}) collective-permute-start(bf16[256,1024]{1,0:T(8,128)(2,1)} %get-tuple-element.113), channel_id=1, source_target_pairs={{2,4},{3,5},{4,6},{5,7},{10,12},{11,13},{12,14},{13,15},{18,20},{1... | collective-permute-start | bytes 1572872 | tf_op jit(solution)/shard_map/ppermute | solution.py:318
  354.5 34.2 %collective-permute-start.31 = (bf16[256,1024]{1,0:T(8,128)(2,1)}, bf16[256,1024]{1,0:T(8,128)(2,1)}, u32[]{:S(2)}, u32[]{:S(2)}) collective-permute-start(bf16[256,1024]{1,0:T(8,128)(2,1)} %get-tuple-element.124), channel_id=1, source_target_pairs={{0,4},{1,5},{6,2},{7,3},{8,12},{9,13},{14,10},{15,11},{16,20},{17,... | collective-permute-start | bytes 1572872 | tf_op jit(solution)/shard_map/ppermute | solution.py:318
  355.8 11.0 %copy-start.6 = (f32[1,512,2048]{2,1,0:T(8,128)S(1)}, f32[1,512,2048]{2,1,0:T(8,128)}, u32[]{:S(2)}) copy-start(f32[1,512,2048]{2,1,0:T(8,128)} %param.12) | copy-start | bytes 12582916
  357.7 32.5 %collective-permute-start.27 = (bf16[256,1024]{1,0:T(8,128)(2,1)}, bf16[256,1024]{1,0:T(8,128)(2,1)}, u32[]{:S(2)}, u32[]{:S(2)}) collective-permute-start(bf16[256,1024]{1,0:T(8,128)(2,1)} %get-tuple-element.107), channel_id=1, source_target_pairs={{2,0},{3,1},{4,2},{5,3},{10,8},{11,9},{12,10},{13,11},{18,16},{19,... | collective-permute-start | bytes 1572872 | tf_op jit(solution)/shard_map/ppermute | solution.py:318
  363.0 37.0 %collective-permute-start.28 = (bf16[256,1024]{1,0:T(8,128)(2,1)}, bf16[256,1024]{1,0:T(8,128)(2,1)}, u32[]{:S(2)}, u32[]{:S(2)}) collective-permute-start(bf16[256,1024]{1,0:T(8,128)(2,1)} %get-tuple-element.108), channel_id=1, source_target_pairs={{2,4},{3,5},{4,6},{5,7},{10,12},{11,13},{12,14},{13,15},{18,20},{1... | collective-permute-start | bytes 1572872 | tf_op jit(solution)/shard_map/ppermute | solution.py:318
  365.2 34.8 %collective-permute-start.26 = (bf16[256,1024]{1,0:T(8,128)(2,1)}, bf16[256,1024]{1,0:T(8,128)(2,1)}, u32[]{:S(2)}, u32[]{:S(2)}) collective-permute-start(bf16[256,1024]{1,0:T(8,128)(2,1)} %get-tuple-element.121), channel_id=1, source_target_pairs={{0,4},{1,5},{6,2},{7,3},{8,12},{9,13},{14,10},{15,11},{16,20},{17,... | collective-permute-start | bytes 1572872 | tf_op jit(solution)/shard_map/ppermute | solution.py:318
  390.1 11.7 %copy-start.8 = (f32[1,256,2048]{2,1,0:T(8,128)S(1)}, f32[1,256,2048]{2,1,0:T(8,128)}, u32[]{:S(2)}) copy-start(f32[1,256,2048]{2,1,0:T(8,128)} %param.13) | copy-start | bytes 6291460
  390.1 11.7 %copy-start.11 = (f32[1,256,2048]{2,1,0:T(8,128)S(1)}, f32[1,256,2048]{2,1,0:T(8,128)}, u32[]{:S(2)}) copy-start(f32[1,256,2048]{2,1,0:T(8,128)} %param.15) | copy-start | bytes 6291460
  (11 other events, 18.0 us)
